TPU v7x, 256 devices: a whole 4x4x8 slice. The times are simulated.
256 devices in a mesh: dp: 16 (over y, z_hi, core), expert: 16 (over x, z_lo).
Axes of the slice: x: 4, y: 4, z: 8 (z_hi: 2, z_lo: 4; z = z_hi * 4 + z_lo), core: 2. Of those that a mesh axis runs over, the one named last changes fastest.
Arguments:
- tokens: bfloat16 [512, 4096], P('dp'), may hold values from -6 to 6
- cotangent: bfloat16 [512, 4096], P('dp'), may hold values from -0.29882812 to 0.29882812
- logits: float32 [512, 64], P('dp'), may hold values from 0 to 320
- routes: int32 [512, 8], P('dp'), may hold values from 0 to 63, as said below
- gate_weight: bfloat16 [64, 1536, 4096], P('expert', 'dp'), may hold values from -0.09375 to 0.09375
- up_weight: bfloat16 [64, 1536, 4096], P('expert', 'dp'), may hold values from -0.09375 to 0.09375
- down_weight: bfloat16 [64, 1536, 4096], P('expert', 'dp'), may hold values from -0.15625 to 0.15625
Outputs:
- logit_grad: float32 [512, 64], P('dp')
- router_grad: float32 [4096, 64], P('dp')
Inputs may be any that keep to these rules, and one draw needn't show every extreme that they name: `routes`: each row names 8 different experts.
All inputs are finite; a program needn't handle non-finite values.
Results may differ from a plain program's by a relative error of at most 0.0028.
Values may be sent and summed in bfloat16 or wider, within the bound.
A program may use at most 64 MiB of HBM per device.

v0:
```python
import jax
import jax.numpy as jnp
from jax import lax
from jax.sharding import PartitionSpec as P


def per_device(tokens, cotangent, logits, routes, gate_weight, up_weight, down_weight):
    data_count = lax.axis_size("dp")
    expert_count = lax.axis_size("expert")
    data_index = lax.axis_index("dp")
    expert_index = lax.axis_index("expert")
    tok_dev = tokens.shape[0]
    local_experts = gate_weight.shape[0]
    ff_dev = gate_weight.shape[1]
    model_width = gate_weight.shape[2]
    unit_count = local_experts * ff_dev
    total_tokens = tok_dev * data_count
    gate_flat = gate_weight.reshape(unit_count, model_width)
    up_flat = up_weight.reshape(unit_count, model_width)
    down_flat = down_weight.reshape(unit_count, model_width)
    contract = (((1,), (1,)), ((), ()))
    rows_x = lax.all_gather(tokens, "dp", axis=0, tiled=True)
    rows_g = lax.all_gather(cotangent, "dp", axis=0, tiled=True)
    row_count = rows_x.shape[0]
    gate_pre = lax.dot_general(rows_x, gate_flat, contract, preferred_element_type=jnp.float32)
    up_pre = lax.dot_general(rows_x, up_flat, contract, preferred_element_type=jnp.float32)
    hidden = jax.nn.silu(gate_pre) * up_pre
    paired = lax.dot_general(rows_g, down_flat, contract, preferred_element_type=jnp.float32)
    partial_value = jnp.sum((hidden * paired).reshape(row_count, local_experts, ff_dev), axis=2)
    experts_all = local_experts * expert_count
    placed = lax.dynamic_update_slice(
        jnp.zeros((total_tokens, experts_all), jnp.float32),
        partial_value,
        (0, expert_index * local_experts),
    )
    summed = lax.psum(placed, ("dp", "expert"))
    scores = lax.dynamic_slice_in_dim(summed, data_index * tok_dev, tok_dev, 0)
    shifted = logits - jnp.max(logits, axis=1, keepdims=True)
    raised = jnp.exp(shifted)
    probs = raised / jnp.sum(raised, axis=1, keepdims=True)
    experts_range = jnp.arange(experts_all, dtype=jnp.int32)
    chosen = jnp.sum(
        (routes[:, :, None] == experts_range[None, None, :]).astype(jnp.float32), axis=1
    )
    mass = jnp.sum(probs * chosen, axis=1, keepdims=True)
    weighted = jnp.sum(probs * chosen * scores, axis=1, keepdims=True)
    prob_grad = scores / mass - chosen * weighted / (mass * mass)
    logit_grad = probs * (prob_grad - jnp.sum(probs * prob_grad, axis=1, keepdims=True))
    grad_bf = logit_grad.astype(jnp.bfloat16)
    router_grad = lax.psum_scatter(
        lax.dot_general(
            tokens, grad_bf, (((0,), (0,)), ((), ())), preferred_element_type=jnp.float32
        ),
        "dp",
        scatter_dimension=0,
        tiled=True,
    )
    return (logit_grad, router_grad)


def solution(mesh):
    placed = (
        P("dp", None),
        P("dp", None),
        P("dp", None),
        P("dp", None),
        P("expert", "dp", None),
        P("expert", "dp", None),
        P("expert", "dp", None),
    )
    return jax.shard_map(
        per_device,
        mesh=mesh,
        in_specs=placed,
        out_specs=(P("dp", None), P("dp", None)),
        check_vma=False,
    )
```

profile of v0, /device:TPU:2, one launch (start us, length us, event | category | flops | bytes accessed | tf_op | source)
XLA Modules:
  0.0 512.4 jit_solution(8383287695367049538)
XLA Ops:
  7.2 0.0 copy-start
  7.2 0.0 all-gather.3.cloned.1.call-start
  7.2 0.7 all-gather.3.cloned.1.call-update
  7.9 0.0 all-gather.5.cloned.1.call-start
  8.0 0.7 all-gather.5.cloned.1.call-update
  8.7 0.0 all-reduce.2.cloned.1.call-start
  8.7 0.8 copy.13
  9.5 0.8 reduce_max.9
  10.3 0.1 convert_reduce_fusion
  10.4 80.5 %all-gather.3.cloned.1.call-done = bf16[512,4096]{1,0:T(8,128)(2,1)} async-done(((bf16[32,4096]{1,0:T(8,128)(2,1)}), bf16[512,4096]{1,0:T(8,128)(2,1)}) %all-gather.3.cloned.1.call-update) | async-done | bytes 4194320 | tf_op jit(solution)/shard_map/all_gather | solution.py:22
  91.0 0.0 copy-done
  91.0 0.0 copy-start.3
  91.0 0.0 copy-start.4
  91.0 4.1 fusion.3
  95.1 0.0 copy-done.3
  95.2 0.3 copy-done.4
  95.4 2.7 convolution_multiply_fusion.1
  98.2 68.4 %all-gather.5.cloned.1.call-done = bf16[512,4096]{1,0:T(8,128)(2,1)} async-done(((bf16[32,4096]{1,0:T(8,128)(2,1)}), bf16[512,4096]{1,0:T(8,128)(2,1)}) %all-gather.5.cloned.1.call-update) | async-done | bytes 4194320 | tf_op jit(solution)/shard_map/all_gather | solution.py:23
  166.5 0.0 copy-start.1
  166.5 6.0 %convolution_multiply_fusion = f32[512,384]{0,1:T(8,128)} fusion(f32[512,384]{0,1:T(8,128)} %convolution_multiply_fusion.1, bf16[512,4096]{1,0:T(8,128)(2,1)} %all-gather.5.cloned.1.call-done, bf16[384,4096]{1,0:T(8,128)(2,1)} %bitcast.16), kind=kOutput, calls=%fused_computation.1 | convolution fusion | flops 1610809344 | bytes 8912896 | tf_op jit(solution)/shard_map/dot_general | solution.py:28
  172.5 1.2 reduce_sum.55
  173.7 0.1 copy.12
  173.9 0.7 broadcast_in_dim.2
  174.6 1.9 dynamic_update_slice.3
  176.5 0.0 all-reduce.2.cloned.1.call-update
  176.5 0.0 reduce-scatter.2.cloned.1.call-start
  176.6 0.0 copy-done.1
  176.6 0.2 fusion.1
  176.8 245.8 %all-reduce.2.cloned.1.call-done = f32[512,64]{1,0:T(8,128)} async-done(((f32[512,64]{1,0:T(8,128)}), f32[512,64]{1,0:T(8,128)}) %all-reduce.2.cloned.1.call-update) | async-done | bytes 131088 | tf_op jit(solution)/shard_map/psum | solution.py:36
  422.5 0.9 multiply_reduce_fusion.1
  423.4 0.9 multiply_reduce_fusion
  424.4 0.1 subtract_multiply_fusion
  424.5 0.0 copy-start.2
  424.5 2.3 convolution_bitcast_fusion
  426.7 0.0 reduce-scatter.2.cloned.1.call-update
  426.8 79.1 %reduce-scatter.2.cloned.1.call-done = f32[256,64]{0,1:T(8,128)} async-done(((f32[4096,64]{0,1:T(8,128)}), f32[256,64]{0,1:T(8,128)}) %reduce-scatter.2.cloned.1.call-update) | async-done | bytes 65552 | tf_op jit(solution)/shard_map/reduce_scatter | solution.py:50
  505.9 0.0 copy-done.2
  (1 shorter events, 0.0 us)
Async XLA Ops:
  7.2 83.8 %copy-start = (bf16[4,96,4096]{2,1,0:T(8,128)(2,1)S(1)}, bf16[4,96,4096]{2,1,0:T(8,128)(2,1)}, u32[]{:S(2)}) copy-start(bf16[4,96,4096]{2,1,0:T(8,128)(2,1)} %param.11) | copy-start | bytes 9437188
  7.2 83.8 %all-gather.3.cloned.1.call-start = ((), (), s32[]{:S(2)}) async-start(), calls=%async_computation.1 | async-start | bytes 4456448 | tf_op jit(solution)/shard_map/all_gather | solution.py:22
  7.9 158.6 %all-gather.5.cloned.1.call-start = ((), (), s32[]{:S(2)}) async-start(), calls=%async_computation.2 | async-start | bytes 4456448 | tf_op jit(solution)/shard_map/all_gather | solution.py:23
  8.7 413.9 %all-reduce.2.cloned.1.call-start = ((), (), s32[]{:S(2)}) async-start(), calls=%async_computation.3 | async-start | bytes 524288 | tf_op jit(solution)/shard_map/psum | solution.py:36
  91.0 4.2 copy-start.3
  91.0 4.4 copy-start.4
  166.5 10.0 %copy-start.1 = (f32[32,64]{1,0:T(8,128)S(1)}, f32[32,64]{1,0:T(8,128)}, u32[]{:S(2)}) copy-start(f32[32,64]{1,0:T(8,128)} %param.9) | copy-start | bytes 24580
  176.5 329.3 %reduce-scatter.2.cloned.1.call-start = ((), (), s32[]{:S(2)}) async-start(), calls=%async_computation.4 | async-start | bytes 1114112 | tf_op jit(solution)/shard_map/reduce_scatter | solution.py:50
  424.5 81.4 %copy-start.2 = (f32[32,64]{1,0:T(8,128)}, f32[32,64]{1,0:T(8,128)S(1)}, u32[]{:S(2)}) copy-start(f32[32,64]{1,0:T(8,128)S(1)} %subtract_multiply_fusion) | copy-start | bytes 24580
Sparse Core Ops, SparseCore 0:
  10.7 80.2 all-gather.2
  93.7 72.8 all-gather.4
  176.6 245.8 all-reduce.1
  427.1 78.7 reduce-scatter.1
where the time goes:
time: 513 us; the launch traced here: 512 us
  waiting for transfers between devices  475 us (93%)
  matrix products  15.1 us (3%)
  between operations  13.8 us (3%)
    psum x1, waiting for transfers between devices, per_device(): summed = lax.psum(placed, ('dp', 'expert'))  246 us
    all_gather x1, waiting for transfers between devices, per_device(): rows_x = lax.all_gather(tokens, 'dp', axis=0, tiled=True)  80.5 us
    reduce_scatter x1, waiting for transfers between devices, per_device(): lax.psum_scatter(lax.dot_general(tokens, grad_bf, (((0,), (0,)), ((), ())...  79.1 us
    all_gather x1, waiting for transfers between devices, per_device(): rows_g = lax.all_gather(cotangent, 'dp', axis=0, tiled=True)  68.4 us
  transfers between devices with their start and end apart: 4, of which 4 were waited for; matrix products, arithmetic and copies ran while one was open for 2% of the time, Pallas kernels for 0%

commit v1 on v0

v1 whole, which is shorter than its diff:
```python
import jax
import jax.numpy as jnp
from jax import lax
from jax.experimental import pallas as pl
from jax.experimental.pallas import tpu as pltpu
from jax.sharding import PartitionSpec as P

MESH = pl.DeviceIdType.MESH
MIB = 1024 * 1024
NT = (((1,), (1,)), ((), ()))


class Sems:
    def __init__(self, ref):
        self.ref, self.names = ref, {}

    def __getitem__(self, name):
        return self.ref.at[self.names.setdefault(name, len(self.names))]


def kernel(tok, cot, logits, routes, gate, up, down, lg_out, rg_out,
           xg, wgu, wd, accx, accg, lmat, probs, chosen, part, got1, got2, lgc, turned,
           load_sem, send_ref, recv_ref):
    d = lax.axis_index("dp")
    e = lax.axis_index("expert")
    y, zh, c = d // 4, (d // 2) % 2, d % 2
    x, zl = e // 4, e % 4
    z = zh * 4 + zl
    par = x % 2
    send_sem, recv_sem = Sems(send_ref), Sems(recv_ref)

    def dev(x_, y_, z_, c_):
        return ((y_ * 2 + z_ // 4) * 2 + c_, x_ * 4 + z_ % 4)

    xp, xm = dev((x + 1) % 4, y, z, c), dev((x + 3) % 4, y, z, c)
    yp, ym = dev(x, (y + 1) % 4, z, c), dev(x, (y + 3) % 4, z, c)
    zp, zm = dev(x, y, (z + 1) % 8, c), dev(x, y, (z + 7) % 8, c)
    low = zl < 2
    outn = tuple(jnp.where(low, a, b) for a, b in zip(zm, zp))
    inn = tuple(jnp.where(low, a, b) for a, b in zip(zp, zm))
    sib = dev(x, y, z, 1 - c)
    edge = (zl == 0) | (zl == 3)

    own_x = pltpu.make_async_copy(tok, xg.at[0, zh, c, y], load_sem.at[0])
    own_g = pltpu.make_async_copy(cot, xg.at[1, zh, c, y], load_sem.at[1])
    w_gate = pltpu.make_async_copy(gate, wgu.at[pl.ds(0, 384)], load_sem.at[2])
    w_up = pltpu.make_async_copy(up, wgu.at[pl.ds(384, 384)], load_sem.at[3])
    w_down = pltpu.make_async_copy(down, wd, load_sem.at[4])
    own_x.start()
    own_g.start()
    barrier = pltpu.get_barrier_semaphore()
    for k in range(1, 16):
        pl.semaphore_signal(barrier, inc=1, device_id=((d + k) % 16, e), device_id_type=MESH)
    for k in range(1, 16):
        pl.semaphore_signal(barrier, inc=1, device_id=(d, (e + k) % 16), device_id_type=MESH)
    for to in (zp, zm):
        pl.semaphore_signal(barrier, inc=1, device_id=to, device_id_type=MESH)
    w_gate.start()
    w_up.start()
    w_down.start()
    lane = lax.broadcasted_iota(jnp.int32, (32, 128), 1)
    picked = jnp.zeros((32, 128), jnp.float32)
    for k in range(8):
        picked += (routes[:, k : k + 1] == lane - 64).astype(jnp.float32)
    lmat[zh, c, y] = picked
    lmat[zh, c, y, :, pl.ds(0, 64)] = logits[...]
    own_x.wait()
    own_g.wait()
    pl.semaphore_wait(barrier, 32)

    pending = []

    def ship(ref, to, name_here, name_there):
        cp = pltpu.make_async_remote_copy(
            ref, ref, send_sem[name_here], recv_sem[name_there], device_id=to, device_id_type=MESH)
        cp.start()
        return cp

    def send(ref, to, name_here, name_there):
        pending.append(ship(ref, to, name_here, name_there))

    def landed(ref, name):
        pltpu.make_async_remote_copy(
            ref, ref, send_sem[("x+", 0, "m", 0)], recv_sem[name], device_id=sib, device_id_type=MESH).wait_recv()

    def piece(dz, dy, rel, s):
        zz = zh if dz == 0 else 1 - zh
        q = 2 * (s % 2) + (par if rel == 0 else 1 - par)
        return xg.at[s // 2, zz, c, (y + dy) % 4, :, pl.ds(pl.multiple_of(q * 1024, 1024), 1024)]

    def group(dz, rel, s, cc):
        zz = zh if dz == 0 else 1 - zh
        q = 2 * (s % 2) + (par if rel == 0 else 1 - par)
        return xg.at[s // 2, zz, cc, :, :, pl.ds(pl.multiple_of(q * 1024, 1024), 1024)]

    DY = {"m": 3, "p": 1, "2": 2}

    def spread_y(dz, s):
        ref = piece(dz, 0, 0, s)
        send(ref, yp, ("y+", dz, s), ("y", dz, "m", s))
        send(ref, ym, ("y-", dz, s), ("y", dz, "p", s))

    def share_x(dz, who, s):
        ref = piece(dz, DY[who], 0, s)
        forward = {"m": True, "p": False, "2": s % 2 == 0}[who]
        forward = forward if s < 2 else not forward
        send(ref, xp if forward else xm, ("x+", dz, who, s), ("x", dz, who, s))

    def on_y(dz, who, s):
        landed(piece(dz, DY[who], 0, s), ("y", dz, who, s))
        if who == "m" and s % 2 == 0:
            send(piece(dz, DY[who], 0, s), yp, ("y2", dz, s), ("y", dz, "2", s))
        if who == "p" and s % 2 == 1:
            send(piece(dz, DY[who], 0, s), ym, ("y2", dz, s), ("y", dz, "2", s))
        share_x(dz, who, s)

    def on_x(dz, who, s):
        landed(piece(dz, DY[who], 1, s), ("x", dz, who, s))

    def at_edge(ref, to, name_here, name_there):
        cp = pltpu.make_async_remote_copy(
            ref, ref, send_sem[name_here], recv_sem[name_there], device_id=to, device_id_type=MESH)
        pl.when(edge)(cp.start)
        edge_pending.append(cp)

    edge_pending = []

    def on_z(rel, s):
        ref = piece(1, 0, rel, s)
        landed(ref, ("z", rel, s))
        at_edge(ref, inn, ("zi", rel, s), ("z", rel, s))
        if rel == 0:
            spread_y(1, s)

    def to_sibling(dz, rel, s):
        send(group(dz, rel, s, c), sib, ("c", dz, rel, s), ("c", dz, rel, s))

    started = set()

    def multiply(dz, rel, s):
        landed(group(dz, rel, s, 1 - c), ("c", dz, rel, s))
        zz = zh if dz == 0 else 1 - zh
        q = 2 * (s % 2) + (par if rel == 0 else 1 - par)
        cols = pl.ds(pl.multiple_of(q * 1024, 1024), 1024)
        arr = s // 2
        rows = xg[arr, zz, :, :, :, cols].reshape(256, 1024)
        w, acc, tiles = (wgu, accx, 3) if arr == 0 else (wd, accg, 3)
        size = 256 if arr == 0 else 128
        for m in range(tiles):
            at = pl.ds(m * size, size)
            value = lax.dot_general(w[at, cols], rows, NT, preferred_element_type=jnp.float32)
            if (dz, arr) in started:
                acc[dz, at, :] += value
            else:
                acc[dz, at, :] = value
        started.add((dz, arr))

    def lblock(dz, dy):
        return lmat.at[zh if dz == 0 else 1 - zh, c, (y + dy) % 4]

    def l_spread(dz):
        send(lblock(dz, 0), yp, ("ly+", dz), ("ly", dz, "m"))
        send(lblock(dz, 0), ym, ("ly-", dz), ("ly", dz, "p"))

    def l_on_y(dz):
        landed(lblock(dz, 3), ("ly", dz, "m"))
        send(lblock(dz, 3), yp, ("ly2", dz), ("ly", dz, "2"))
        landed(lblock(dz, 1), ("ly", dz, "p"))

    def l_sibling(dz):
        landed(lblock(dz, 2), ("ly", dz, "2"))
        zz = zh if dz == 0 else 1 - zh
        ref = lmat.at[zz, c]
        send(ref, sib, ("lc", dz), ("lc", dz))

    def l_done(dz):
        zz = zh if dz == 0 else 1 - zh
        landed(lmat.at[zz, 1 - c], ("lc", dz))

    for s in range(4):
        spread_y(0, s)
        at_edge(piece(0, 0, 0, s), outn, ("zo", 0, s), ("z", 0, s))
        if s == 0:
            l_spread(0)
            at_edge(lblock(0, 0), outn, ("lzo",), ("lz",))
    for s in range(4):
        at_edge(piece(0, 0, 1, s), outn, ("zo", 1, s), ("z", 1, s))
    w_gate.wait()
    w_up.wait()
    w_down.wait()
    l_on_y(0)
    for s in range(4):
        on_y(0, "m", s)
        on_y(0, "p", s)
        if s == 1:
            landed(lblock(1, 0), ("lz",))
            at_edge(lblock(1, 0), inn, ("lzi",), ("lz",))
            l_spread(1)
            l_sibling(0)
        if s >= 1:
            on_z(0, s - 1)
    on_z(0, 3)
    for s in range(4):
        landed(piece(0, 2, 0, s), ("y", 0, "2", s))
        share_x(0, "2", s)
        to_sibling(0, 0, s)
    l_on_y(1)
    for s in range(4):
        on_x(0, "m", s)
        on_x(0, "p", s)
    for s in range(2):
        on_y(1, "m", s)
        on_y(1, "p", s)
    l_sibling(1)
    multiply(0, 0, 0)
    for s in range(2):
        on_z(1, s)
        on_y(1, "m", s + 2)
        on_y(1, "p", s + 2)
    multiply(0, 0, 1)
    for s in range(4):
        on_x(0, "2", s)
        to_sibling(0, 1, s)
    on_z(1, 2)
    on_z(1, 3)
    multiply(0, 0, 2)
    multiply(0, 0, 3)

    l_done(0)
    l_done(1)
    half = lax.broadcasted_iota(jnp.int32, (8, 256), 0) < 4

    def over_experts(v, op, fold):
        t = op(v, axis=0)
        a = op(t[0:4], axis=0, keepdims=True)
        b = op(t[4:8], axis=0, keepdims=True)
        return jnp.where(half, a, b)

    for zz in range(2):
        flipped = lmat[zz].reshape(256, 128).T
        for k in range(16):
            probs[k, pl.ds(zz * 4, 4), :] = flipped[k * 4 : k * 4 + 4]
            chosen[k, pl.ds(zz * 4, 4), :] = flipped[64 + k * 4 : 68 + k * 4]
    raw = probs[...]
    raised = jnp.exp(raw - over_experts(raw, jnp.max, None))
    probs[...] = raised / over_experts(raised, jnp.sum, None)

    for s in range(4):
        landed(piece(1, 2, 0, s), ("y", 1, "2", s))
        share_x(1, "2", s)
        to_sibling(1, 0, s)
        multiply(0, 1, s)
    for s in range(4):
        on_x(1, "m", s)
        on_x(1, "p", s)
        on_x(1, "2", s)
        to_sibling(1, 1, s)
        multiply(1, 0, s)
    for s in range(4):
        multiply(1, 1, s)

    def local_scores(dz):
        g = accx[dz, 0:384, :]
        hidden = g / (1.0 + jnp.exp(-g)) * accx[dz, 384:768, :]
        both = hidden * accg[dz]
        return jnp.concatenate([jnp.sum(both[k * 96 : k * 96 + 96], axis=0, keepdims=True) for k in range(4)], axis=0)

    here, there = local_scores(0), local_scores(1)
    part[...] = jnp.where(zh == 0, jnp.concatenate([here, there], 0), jnp.concatenate([there, here], 0))

    sends = []
    for k in range(1, 16):
        to = (d + k) % 16
        cp = pltpu.make_async_remote_copy(
            part, got1.at[k], send_sem[("s1", k)], recv_sem[("s1", k)], device_id=(to, e), device_id_type=MESH)
        cp.start()
        sends.append(cp)
    total = part[...]
    for k in range(1, 16):
        sends[k - 1].wait_recv()
        total += got1[k]
    got2[e] = total
    sends2 = []
    for k in range(1, 16):
        to = (e + k) % 16
        mine = got2.at[e]
        cp = pltpu.make_async_remote_copy(
            mine, mine, send_sem[("s2", k)], recv_sem[("s2", k)], device_id=(d, to), device_id_type=MESH)
        cp.start()
        sends2.append(cp)
    for k in range(1, 16):
        theirs = got2.at[(e + 16 - k) % 16]
        pltpu.make_async_remote_copy(
            theirs, theirs, send_sem[("s2", k)], recv_sem[("s2", k)], device_id=sib, device_id_type=MESH).wait_recv()

    scores = got2[...]
    pr, ch = probs[...], chosen[...]
    kept = pr * ch
    mass = over_experts(kept, jnp.sum, None)
    weighted = over_experts(kept * scores, jnp.sum, None)
    prob_grad = scores / mass - ch * (weighted / (mass * mass))
    grad = pr * (prob_grad - over_experts(pr * prob_grad, jnp.sum, None))
    for k in range(16):
        lgc[0, pl.ds(k * 4, 4), :] = grad[k, 0:4]
        lgc[1, pl.ds(k * 4, 4), :] = grad[k, 4:8]
    turned[...] = lgc[zh].T
    lg_out[...] = turned[pl.ds(c * 128 + y * 32, 32), :]
    cols = pl.ds(pl.multiple_of(d * 256, 256), 256)
    rg = jnp.zeros((64, 256), jnp.float32)
    for zz in range(2):
        rows = xg[0, zz, :, :, :, cols].reshape(256, 256)
        rg += jnp.dot(lgc[zz].astype(jnp.bfloat16), rows, preferred_element_type=jnp.float32)
    rg_out[...] = rg.T

    for cp in pending + sends + sends2:
        cp.wait_send()

    @pl.when(edge)
    def _():
        for cp in edge_pending:
            cp.wait_send()


N_SEND, N_RECV = 160, 128


def per_device(tokens, cotangent, logits, routes, gate_weight, up_weight, down_weight):
    flat = [w.reshape(384, 4096) for w in (gate_weight, up_weight, down_weight)]
    hbm, vmem = pl.BlockSpec(memory_space=pl.ANY), pl.BlockSpec(memory_space=pltpu.VMEM)
    f32, bf16 = jnp.float32, jnp.bfloat16
    return pl.pallas_call(
        kernel,
        out_shape=(jax.ShapeDtypeStruct((32, 64), f32), jax.ShapeDtypeStruct((256, 64), f32)),
        in_specs=[hbm, hbm, vmem, vmem, hbm, hbm, hbm],
        out_specs=(vmem, vmem),
        scratch_shapes=[
            pltpu.VMEM((2, 2, 2, 4, 32, 4096), bf16),
            pltpu.VMEM((768, 4096), bf16),
            pltpu.VMEM((384, 4096), bf16),
            pltpu.VMEM((2, 768, 256), f32),
            pltpu.VMEM((2, 384, 256), f32),
            pltpu.VMEM((2, 2, 4, 32, 128), f32),
            pltpu.VMEM((16, 8, 256), f32),
            pltpu.VMEM((16, 8, 256), f32),
            pltpu.VMEM((8, 256), f32),
            pltpu.VMEM((16, 8, 256), f32),
            pltpu.VMEM((16, 8, 256), f32),
            pltpu.VMEM((2, 64, 256), f32),
            pltpu.VMEM((256, 64), f32),
            pltpu.SemaphoreType.DMA((5,)),
            pltpu.SemaphoreType.DMA((N_SEND,)),
            pltpu.SemaphoreType.DMA((N_RECV,)),
        ],
        compiler_params=pltpu.CompilerParams(
            collective_id=0, has_side_effects=True, vmem_limit_bytes=60 * MIB),
        cost_estimate=pl.CostEstimate(flops=2 * 512 * 384 * 4096 * 3, bytes_accessed=10 * MIB, transcendentals=512 * 384),
        name="router_grad",
    )(tokens, cotangent, logits, routes, *flat)


def solution(mesh):
    rows = P("dp", None)
    placed = (rows, rows, rows, rows) + (P("expert", "dp", None),) * 3
    return jax.shard_map(
        per_device, mesh=mesh, in_specs=placed, out_specs=(rows, rows), check_vma=False)
```

time: 513 us -> 66.5 us (0.13)
  waiting for transfers between devices: 475 us -> 0 us
  Pallas kernels: 0 us -> 60.2 us
  matrix products: 15.1 us -> 0 us
  between operations: 13.8 us -> 0.64 us
    psum x1 -> x0, waiting for transfers between devices: 246 us -> none  [per_device(): summed = lax.psum(placed, ('dp', 'expert'))]
    all_gather x2 -> x0, waiting for transfers between devices: 149 us -> none  [the longest x1 80.5 us: per_device(): rows_x = lax.all_gather(tokens, 'dp', axis=0, tiled=True)]
    reduce_scatter x1 -> x0, waiting for transfers between devices: 79.1 us -> none  [per_device(): lax.psum_scatter(lax.dot_general(tokens, grad_bf, (((0,), (0,)), ((), ())...]
    pallas_call x0 -> x1, Pallas kernels: none -> 60.2 us  [per_device(): pl.pallas_call(kernel, out_shape=(jax.ShapeDtypeStruct((32, 64), f32), ja...]
    dot_general x4 -> x0, matrix products: 15.1 us -> none  [the longest x1 5.99 us: per_device(): lax.dot_general(rows_g, down_flat, contract, preferred_element_type=jnp.f...]
  transfers between devices with their start and end apart: 4 -> 0, of which waited for: 4 -> 0; matrix products, arithmetic and copies ran while one was open for 2% -> 0% of each run, Pallas kernels for 0% -> 0%
where the time goes in v1:
time: 66.5 us; the launch traced here: 65.2 us
  Pallas kernels  60.2 us (91%)
  local copies, waits for them, and re-layouts  4.31 us (6%)
    pallas_call x1, Pallas kernels, per_device(): pl.pallas_call(kernel, out_shape=(jax.ShapeDtypeStruct((32, 64), f32), ja...  60.2 us
    unnamed x2, local copies, waits for them, and re-layouts  2.69 us
    pallas_call x1, local copies, waits for them, and re-layouts, per_device(): pl.pallas_call(kernel, out_shape=(jax.ShapeDtypeStruct((32, 64), f32), ja...  1.62 us

profile of v1, /device:TPU:2, one launch (start us, length us, event | category | flops | bytes accessed | tf_op | source)
XLA Modules:
  0.0 65.2 jit_solution(15622809222238712533)
XLA Ops:
  0.6 1.4 %copy.9.routes = s32[32,8]{1,0:T(8,128)} copy(s32[32,8]{0,1:T(8,128)} %param.10) | data formatting | bytes 2048 | tf_op args[3]
  2.0 60.2 %router_grad.1 = (f32[32,64]{1,0:T(8,128)}, f32[256,64]{1,0:T(8,128)}) custom-call(bf16[32,4096]{1,0:T(8,128)(2,1)} %tok.1, bf16[32,4096]{1,0:T(8,128)(2,1)} %cot.1, f32[32,64]{1,0:T(8,128)} %logits.1, s32[32,8]{1,0:T(8,128)} %copy.9.routes, bf16[384,4096]{1,0:T(8,128)(2,1)} %bitcast.3, bf16[384,4096]{1,0:T(8,128)(2,1)} %bitcast.4, bf16[384,4096]{1,0:T(8,128)(2,1)} %bitcast.5), custom_call_target="tpu_custom_call" | custom-call | flops 4831838208 | bytes 10485760 | tf_op jit(solution)/shard_map/router_grad/pallas_call | solution.py:331
  62.2 1.6 %copy.10 = f32[256,64]{0,1:T(8,128)} copy(f32[256,64]{1,0:T(8,128)} %get-tuple-element.3) | data formatting | bytes 131072 | tf_op jit(solution)/shard_map/router_grad/pallas_call | solution.py:331
  63.8 1.3 %copy.12 = f32[32,64]{1,0:T(8,128)} copy(f32[32,64]{1,0:T(8,128)} %get-tuple-element.6) | data formatting | bytes 16384

commit v2 on v1

--- a/solution.py
+++ b/solution.py
@@ -19,8 +19,8 @@
 
 
 def kernel(tok, cot, logits, routes, gate, up, down, lg_out, rg_out,
-           xg, wgu, wd, accx, accg, lmat, probs, chosen, part, got1, got2, lgc, turned,
-           load_sem, send_ref, recv_ref):
+           xg, wgu, wd, accx, accg, lmat, probs, chosen, part, total, got_y, got_z, got2, lgc, turned,
+           load_sem, send_ref, recv_ref, met):
     d = lax.axis_index("dp")
     e = lax.axis_index("expert")
     y, zh, c = d // 4, (d // 2) % 2, d % 2
@@ -46,27 +46,23 @@
     w_gate = pltpu.make_async_copy(gate, wgu.at[pl.ds(0, 384)], load_sem.at[2])
     w_up = pltpu.make_async_copy(up, wgu.at[pl.ds(384, 384)], load_sem.at[3])
     w_down = pltpu.make_async_copy(down, wd, load_sem.at[4])
+    barrier = pltpu.get_barrier_semaphore()
+    for to in (yp, ym, xp, xm, zp, zm, sib):
+        pl.semaphore_signal(barrier, inc=1, device_id=to, device_id_type=MESH)
     own_x.start()
     own_g.start()
-    barrier = pltpu.get_barrier_semaphore()
-    for k in range(1, 16):
-        pl.semaphore_signal(barrier, inc=1, device_id=((d + k) % 16, e), device_id_type=MESH)
-    for k in range(1, 16):
-        pl.semaphore_signal(barrier, inc=1, device_id=(d, (e + k) % 16), device_id_type=MESH)
-    for to in (zp, zm):
-        pl.semaphore_signal(barrier, inc=1, device_id=to, device_id_type=MESH)
     w_gate.start()
     w_up.start()
     w_down.start()
-    lane = lax.broadcasted_iota(jnp.int32, (32, 128), 1)
-    picked = jnp.zeros((32, 128), jnp.float32)
+    expert = lax.broadcasted_iota(jnp.int32, (64, 32), 0)
+    picked = jnp.zeros((64, 32), jnp.float32)
     for k in range(8):
-        picked += (routes[:, k : k + 1] == lane - 64).astype(jnp.float32)
-    lmat[zh, c, y] = picked
+        picked += (routes[k : k + 1, :] == expert).astype(jnp.float32)
     lmat[zh, c, y, :, pl.ds(0, 64)] = logits[...]
+    lmat[zh, c, y, :, pl.ds(64, 64)] = picked.T
     own_x.wait()
     own_g.wait()
-    pl.semaphore_wait(barrier, 32)
+    pl.semaphore_wait(barrier, 7)
 
     pending = []
 
@@ -117,20 +113,27 @@
     def on_x(dz, who, s):
         landed(piece(dz, DY[who], 1, s), ("x", dz, who, s))
 
+    edge_pending = []
+
     def at_edge(ref, to, name_here, name_there):
         cp = pltpu.make_async_remote_copy(
             ref, ref, send_sem[name_here], recv_sem[name_there], device_id=to, device_id_type=MESH)
         pl.when(edge)(cp.start)
         edge_pending.append(cp)
 
-    edge_pending = []
-
-    def on_z(rel, s):
+    def z_edge(rel, s):
         ref = piece(1, 0, rel, s)
-        landed(ref, ("z", rel, s))
-        at_edge(ref, inn, ("zi", rel, s), ("z", rel, s))
-        if rel == 0:
-            spread_y(1, s)
+        on = pltpu.make_async_remote_copy(
+            ref, ref, send_sem[("zi", rel, s)], recv_sem[("z", rel, s)], device_id=inn, device_id_type=MESH)
+        edge_pending.append(on)
+
+        @pl.when(edge)
+        def _():
+            landed(ref, ("z", rel, s))
+            on.start()
+
+    def z_inner(rel, s):
+        pl.when(~edge)(lambda: landed(piece(1, 0, rel, s), ("z", rel, s)))
 
     def to_sibling(dz, rel, s):
         send(group(dz, rel, s, c), sib, ("c", dz, rel, s), ("c", dz, rel, s))
@@ -144,10 +147,9 @@
         cols = pl.ds(pl.multiple_of(q * 1024, 1024), 1024)
         arr = s // 2
         rows = xg[arr, zz, :, :, :, cols].reshape(256, 1024)
-        w, acc, tiles = (wgu, accx, 3) if arr == 0 else (wd, accg, 3)
-        size = 256 if arr == 0 else 128
-        for m in range(tiles):
-            at = pl.ds(m * size, size)
+        w, acc, tiles = (wgu, accx, (0, 256, 512)) if arr == 0 else (wd, accg, (0, 256))
+        for m in tiles:
+            at = pl.ds(m, min(256, w.shape[0] - m))
             value = lax.dot_general(w[at, cols], rows, NT, preferred_element_type=jnp.float32)
             if (dz, arr) in started:
                 acc[dz, at, :] += value
@@ -177,60 +179,123 @@
         zz = zh if dz == 0 else 1 - zh
         landed(lmat.at[zz, 1 - c], ("lc", dz))
 
+    def greet(k):
+        pl.semaphore_signal(met.at[2 * k], inc=1, device_id=zp, device_id_type=MESH)
+        pl.semaphore_signal(met.at[2 * k + 1], inc=1, device_id=zm, device_id_type=MESH)
+
+    def greeted(k):
+        pl.semaphore_wait(met.at[2 * k], 1)
+        pl.semaphore_wait(met.at[2 * k + 1], 1)
+
+    def on_y_both(dz, s):
+        on_y(dz, "m", s)
+        on_y(dz, "p", s)
+
+    def on_y2(dz, s):
+        landed(piece(dz, 2, 0, s), ("y", dz, "2", s))
+        share_x(dz, "2", s)
+        to_sibling(dz, 0, s)
+
+    def on_x_all(dz, s):
+        on_x(dz, "m", s)
+        on_x(dz, "p", s)
+        on_x(dz, "2", s)
+        to_sibling(dz, 1, s)
+
+    def l_edge():
+        on = pltpu.make_async_remote_copy(
+            lblock(1, 0), lblock(1, 0), send_sem[("lzi",)], recv_sem[("lz",)], device_id=inn, device_id_type=MESH)
+        edge_pending.append(on)
+
+        @pl.when(edge)
+        def _():
+            landed(lblock(1, 0), ("lz",))
+            on.start()
+
+    def l_on_z():
+        pl.when(~edge)(lambda: landed(lblock(1, 0), ("lz",)))
+        l_spread(1)
+
+    l_spread(0)
+    at_edge(lblock(0, 0), outn, ("lzo",), ("lz",))
     for s in range(4):
         spread_y(0, s)
         at_edge(piece(0, 0, 0, s), outn, ("zo", 0, s), ("z", 0, s))
-        if s == 0:
-            l_spread(0)
-            at_edge(lblock(0, 0), outn, ("lzo",), ("lz",))
     for s in range(4):
         at_edge(piece(0, 0, 1, s), outn, ("zo", 1, s), ("z", 1, s))
+    greet(0)
     w_gate.wait()
     w_up.wait()
     w_down.wait()
+    on_y_both(0, 0)
+    l_edge()
+    z_edge(0, 0)
+    on_y_both(0, 1)
+    z_edge(0, 1)
     l_on_y(0)
-    for s in range(4):
-        on_y(0, "m", s)
-        on_y(0, "p", s)
-        if s == 1:
-            landed(lblock(1, 0), ("lz",))
-            at_edge(lblock(1, 0), inn, ("lzi",), ("lz",))
-            l_spread(1)
-            l_sibling(0)
-        if s >= 1:
-            on_z(0, s - 1)
-    on_z(0, 3)
-    for s in range(4):
-        landed(piece(0, 2, 0, s), ("y", 0, "2", s))
-        share_x(0, "2", s)
-        to_sibling(0, 0, s)
+    greeted(0)
+    greet(1)
+    on_y_both(0, 2)
+    z_edge(0, 2)
+    z_inner(0, 0)
+    spread_y(1, 0)
+    on_y_both(0, 3)
+    z_edge(0, 3)
+    z_inner(0, 1)
+    spread_y(1, 1)
+    on_y2(0, 0)
+    z_edge(1, 0)
+    greeted(1)
+    greet(2)
+    on_y2(0, 1)
+    z_inner(0, 2)
+    spread_y(1, 2)
+    z_edge(1, 1)
+    on_y2(0, 2)
+    z_inner(0, 3)
+    spread_y(1, 3)
+    z_edge(1, 2)
+    l_on_z()
+    multiply(0, 0, 0)
+    on_y2(0, 3)
+    z_edge(1, 3)
+    multiply(0, 0, 1)
+    l_sibling(0)
+    on_y_both(1, 0)
+    multiply(0, 0, 2)
+    on_y_both(1, 1)
+    multiply(0, 0, 3)
+    on_x_all(0, 0)
+    on_y_both(1, 2)
     l_on_y(1)
-    for s in range(4):
-        on_x(0, "m", s)
-        on_x(0, "p", s)
-    for s in range(2):
-        on_y(1, "m", s)
-        on_y(1, "p", s)
+    on_x_all(0, 1)
+    multiply(0, 1, 0)
+    on_y_both(1, 3)
+    on_x_all(0, 2)
+    multiply(0, 1, 1)
+    on_y2(1, 0)
+    on_x_all(0, 3)
+    multiply(0, 1, 2)
+    on_y2(1, 1)
+    multiply(0, 1, 3)
+    z_inner(1, 0)
+    z_inner(1, 1)
+    on_y2(1, 2)
+    multiply(1, 0, 0)
+    z_inner(1, 2)
+    z_inner(1, 3)
+    greeted(2)
+    on_y2(1, 3)
     l_sibling(1)
-    multiply(0, 0, 0)
-    for s in range(2):
-        on_z(1, s)
-        on_y(1, "m", s + 2)
-        on_y(1, "p", s + 2)
-    multiply(0, 0, 1)
-    for s in range(4):
-        on_x(0, "2", s)
-        to_sibling(0, 1, s)
-    on_z(1, 2)
-    on_z(1, 3)
-    multiply(0, 0, 2)
-    multiply(0, 0, 3)
+    multiply(1, 0, 1)
+    on_x_all(1, 0)
+    multiply(1, 0, 2)
 
     l_done(0)
     l_done(1)
     half = lax.broadcasted_iota(jnp.int32, (8, 256), 0) < 4
 
-    def over_experts(v, op, fold):
+    def over_experts(v, op):
         t = op(v, axis=0)
         a = op(t[0:4], axis=0, keepdims=True)
         b = op(t[4:8], axis=0, keepdims=True)
@@ -242,22 +307,17 @@
             probs[k, pl.ds(zz * 4, 4), :] = flipped[k * 4 : k * 4 + 4]
             chosen[k, pl.ds(zz * 4, 4), :] = flipped[64 + k * 4 : 68 + k * 4]
     raw = probs[...]
-    raised = jnp.exp(raw - over_experts(raw, jnp.max, None))
-    probs[...] = raised / over_experts(raised, jnp.sum, None)
-
-    for s in range(4):
-        landed(piece(1, 2, 0, s), ("y", 1, "2", s))
-        share_x(1, "2", s)
-        to_sibling(1, 0, s)
-        multiply(0, 1, s)
-    for s in range(4):
-        on_x(1, "m", s)
-        on_x(1, "p", s)
-        on_x(1, "2", s)
-        to_sibling(1, 1, s)
-        multiply(1, 0, s)
-    for s in range(4):
-        multiply(1, 1, s)
+    raised = jnp.exp(raw - over_experts(raw, jnp.max))
+    probs[...] = raised / over_experts(raised, jnp.sum)
+
+    on_x_all(1, 1)
+    multiply(1, 0, 3)
+    on_x_all(1, 2)
+    multiply(1, 1, 0)
+    on_x_all(1, 3)
+    multiply(1, 1, 1)
+    multiply(1, 1, 2)
+    multiply(1, 1, 3)
 
     def local_scores(dz):
         g = accx[dz, 0:384, :]
@@ -268,38 +328,40 @@
     here, there = local_scores(0), local_scores(1)
     part[...] = jnp.where(zh == 0, jnp.concatenate([here, there], 0), jnp.concatenate([there, here], 0))
 
-    sends = []
-    for k in range(1, 16):
-        to = (d + k) % 16
-        cp = pltpu.make_async_remote_copy(
-            part, got1.at[k], send_sem[("s1", k)], recv_sem[("s1", k)], device_id=(to, e), device_id_type=MESH)
-        cp.start()
-        sends.append(cp)
-    total = part[...]
-    for k in range(1, 16):
-        sends[k - 1].wait_recv()
-        total += got1[k]
-    got2[e] = total
-    sends2 = []
-    for k in range(1, 16):
-        to = (e + k) % 16
-        mine = got2.at[e]
-        cp = pltpu.make_async_remote_copy(
-            mine, mine, send_sem[("s2", k)], recv_sem[("s2", k)], device_id=(d, to), device_id_type=MESH)
-        cp.start()
-        sends2.append(cp)
-    for k in range(1, 16):
-        theirs = got2.at[(e + 16 - k) % 16]
+    def exchange(tag, source, place, peers):
+        copies = {}
+        for k, to in peers:
+            copies[k] = pltpu.make_async_remote_copy(
+                source, place(k), send_sem[(tag, k)], recv_sem[(tag, k)], device_id=to, device_id_type=MESH)
+            copies[k].start()
+        pending.extend(copies.values())
+        return copies
+
+    copies = exchange("ty", part, lambda k: got_y.at[k], [
+        (dy * 2 + dc, dev(x, (y + dy) % 4, z, (c + dc) % 2)) for dy, dc in ((2, 1), (2, 0), (1, 1), (3, 1), (1, 0), (3, 0), (0, 1))])
+    for k in (1, 2, 6, 3, 7, 4, 5):
+        copies[k].wait_recv()
+    total[...] = part[...] + sum(got_y[k] for k in range(1, 8))
+    copies = exchange("tz", total, lambda k: got_z.at[k], [(k, dev(x, y, (z + k) % 8, c)) for k in (4, 3, 5, 2, 6, 1, 7)])
+    for k in (1, 7, 2, 6, 3, 5, 4):
+        copies[k].wait_recv()
+    for k in range(4):
+        first = total[...] if k == 0 else got_z[k]
+        got2[x * 4 + (z + 8 - k) % 4] = first + got_z[k + 4]
+    mine = got2.at[pl.ds(x * 4, 4)]
+    copies = exchange("tx", mine, lambda k: mine, [(k, dev((x + k) % 4, y, z, c)) for k in (2, 1, 3)])
+    for k in (1, 3, 2):
+        theirs = got2.at[pl.ds((x + 4 - k) % 4 * 4, 4)]
         pltpu.make_async_remote_copy(
-            theirs, theirs, send_sem[("s2", k)], recv_sem[("s2", k)], device_id=sib, device_id_type=MESH).wait_recv()
+            theirs, theirs, send_sem[("tx", k)], recv_sem[("tx", k)], device_id=sib, device_id_type=MESH).wait_recv()
 
     scores = got2[...]
     pr, ch = probs[...], chosen[...]
     kept = pr * ch
-    mass = over_experts(kept, jnp.sum, None)
-    weighted = over_experts(kept * scores, jnp.sum, None)
+    mass = over_experts(kept, jnp.sum)
+    weighted = over_experts(kept * scores, jnp.sum)
     prob_grad = scores / mass - ch * (weighted / (mass * mass))
-    grad = pr * (prob_grad - over_experts(pr * prob_grad, jnp.sum, None))
+    grad = pr * (prob_grad - over_experts(pr * prob_grad, jnp.sum))
     for k in range(16):
         lgc[0, pl.ds(k * 4, 4), :] = grad[k, 0:4]
         lgc[1, pl.ds(k * 4, 4), :] = grad[k, 4:8]
@@ -310,9 +372,9 @@
     for zz in range(2):
         rows = xg[0, zz, :, :, :, cols].reshape(256, 256)
         rg += jnp.dot(lgc[zz].astype(jnp.bfloat16), rows, preferred_element_type=jnp.float32)
-    rg_out[...] = rg.T
-
-    for cp in pending + sends + sends2:
+    rg_out[...] = rg
+
+    for cp in pending:
         cp.wait_send()
 
     @pl.when(edge)
@@ -328,9 +390,9 @@
     flat = [w.reshape(384, 4096) for w in (gate_weight, up_weight, down_weight)]
     hbm, vmem = pl.BlockSpec(memory_space=pl.ANY), pl.BlockSpec(memory_space=pltpu.VMEM)
     f32, bf16 = jnp.float32, jnp.bfloat16
-    return pl.pallas_call(
+    logit_grad, router_grad = pl.pallas_call(
         kernel,
-        out_shape=(jax.ShapeDtypeStruct((32, 64), f32), jax.ShapeDtypeStruct((256, 64), f32)),
+        out_shape=(jax.ShapeDtypeStruct((32, 64), f32), jax.ShapeDtypeStruct((64, 256), f32)),
         in_specs=[hbm, hbm, vmem, vmem, hbm, hbm, hbm],
         out_specs=(vmem, vmem),
         scratch_shapes=[
@@ -343,19 +405,23 @@
             pltpu.VMEM((16, 8, 256), f32),
             pltpu.VMEM((16, 8, 256), f32),
             pltpu.VMEM((8, 256), f32),
-            pltpu.VMEM((16, 8, 256), f32),
+            pltpu.VMEM((8, 256), f32),
+            pltpu.VMEM((8, 8, 256), f32),
+            pltpu.VMEM((8, 8, 256), f32),
             pltpu.VMEM((16, 8, 256), f32),
             pltpu.VMEM((2, 64, 256), f32),
             pltpu.VMEM((256, 64), f32),
             pltpu.SemaphoreType.DMA((5,)),
             pltpu.SemaphoreType.DMA((N_SEND,)),
             pltpu.SemaphoreType.DMA((N_RECV,)),
+            pltpu.SemaphoreType.REGULAR((6,)),
         ],
         compiler_params=pltpu.CompilerParams(
             collective_id=0, has_side_effects=True, vmem_limit_bytes=60 * MIB),
         cost_estimate=pl.CostEstimate(flops=2 * 512 * 384 * 4096 * 3, bytes_accessed=10 * MIB, transcendentals=512 * 384),
         name="router_grad",
-    )(tokens, cotangent, logits, routes, *flat)
+    )(tokens, cotangent, logits, routes.T, *flat)
+    return logit_grad, router_grad.T
 
 
 def solution(mesh):

time: 66.5 us -> 56.1 us (0.84); the launches traced: 65.2 us -> 55.8 us
  Pallas kernels: 60.2 us -> 52.3 us
  local copies, waits for them, and re-layouts: 4.31 us -> 2.8 us
    pallas_call x1, Pallas kernels: 60.2 us -> 52.3 us  [per_device(): pl.pallas_call(kernel, out_shape=(jax.ShapeDtypeStruct((32, 64), f32), ja...]
    pallas_call x1 -> x0, local copies, waits for them, and re-layouts: 1.62 us -> none  [per_device(): pl.pallas_call(kernel, out_shape=(jax.ShapeDtypeStruct((32, 64), f32), ja...]
where the time goes in v2:
time: 56.1 us; the launch traced here: 55.8 us
  Pallas kernels  52.3 us (93%)
  local copies, waits for them, and re-layouts  2.8 us (5%)
  between operations  0.64 us (1%)
    pallas_call x1, Pallas kernels, per_device(): pl.pallas_call(kernel, out_shape=(jax.ShapeDtypeStruct((32, 64), f32), ja...  52.3 us
    unnamed x2, local copies, waits for them, and re-layouts  2.8 us

profile of v2, /device:TPU:2, one launch (start us, length us, event | category | flops | bytes accessed | tf_op | source)
XLA Modules:
  0.0 55.8 jit_solution(14604124957728255069)
XLA Ops:
  0.6 52.3 %router_grad.1 = (f32[32,64]{1,0:T(8,128)}, f32[64,256]{1,0:T(8,128)}) custom-call(bf16[32,4096]{1,0:T(8,128)(2,1)} %tok.1, bf16[32,4096]{1,0:T(8,128)(2,1)} %cot.1, f32[32,64]{1,0:T(8,128)} %logits.1, s32[8,32]{1,0:T(8,128)} %bitcast.9, bf16[384,4096]{1,0:T(8,128)(2,1)} %bitcast.6, bf16[384,4096]{1,0:T(8,128)(2,1)} %bitcast.7, bf16[384,4096]{1,0:T(8,128)(2,1)} %bitcast.8), custom_call_target="tpu_custom_call" | custom-call | flops 4831838208 | bytes 10485760 | tf_op jit(solution)/shard_map/router_grad/pallas_call | solution.py:393
  53.0 1.3 %copy.11 = f32[32,64]{1,0:T(8,128)} copy(f32[32,64]{1,0:T(8,128)} %get-tuple-element.8) | data formatting | bytes 16384
  54.3 1.5 %copy.12 = f32[256,64]{0,1:T(8,128)} copy(f32[256,64]{0,1:T(8,128)} %bitcast.5) | data formatting | bytes 131072

commit v3 on v2

v3 whole, which is shorter than its diff:
```python
import jax
import jax.numpy as jnp
from jax import lax
from jax.experimental import pallas as pl
from jax.experimental.pallas import tpu as pltpu
from jax.sharding import PartitionSpec as P

MESH = pl.DeviceIdType.MESH
MIB = 1024 * 1024
NT = (((1,), (1,)), ((), ()))


class Sems:
    def __init__(self, ref):
        self.ref, self.names = ref, {}

    def __getitem__(self, name):
        return self.ref.at[self.names.setdefault(name, len(self.names))]


def kernel(tok, cot, logits, routes, gate, up, down, lg_out, rg_out,
           xg, wgu, wd, accx, accg, lmat, probs, chosen, part, total, got_y, got_z, got2, lgc, turned,
           load_sem, send_ref, recv_ref, out_sem, in_sem, met):
    d = lax.axis_index("dp")
    e = lax.axis_index("expert")
    y, zh, c = d // 4, (d // 2) % 2, d % 2
    x, zl = e // 4, e % 4
    z = zh * 4 + zl
    par = x % 2
    send_sem, recv_sem = Sems(send_ref), Sems(recv_ref)

    def dev(x_, y_, z_, c_):
        return ((y_ * 2 + z_ // 4) * 2 + c_, x_ * 4 + z_ % 4)

    xp, xm = dev((x + 1) % 4, y, z, c), dev((x + 3) % 4, y, z, c)
    yp, ym = dev(x, (y + 1) % 4, z, c), dev(x, (y + 3) % 4, z, c)
    zp, zm = dev(x, y, (z + 1) % 8, c), dev(x, y, (z + 7) % 8, c)
    low = zl < 2
    outn = tuple(jnp.where(low, a, b) for a, b in zip(zm, zp))
    inn = tuple(jnp.where(low, a, b) for a, b in zip(zp, zm))
    sib = dev(x, y, z, 1 - c)
    edge = (zl == 0) | (zl == 3)

    barrier = pltpu.get_barrier_semaphore()
    for to in (yp, ym, xp, xm, zp, zm, sib):
        pl.semaphore_signal(barrier, inc=1, device_id=to, device_id_type=MESH)
    own_x = pltpu.make_async_copy(tok, xg.at[0, zh, c, y], load_sem.at[0])
    own_g = pltpu.make_async_copy(cot, xg.at[1, zh, c, y], load_sem.at[1])
    w_gate = pltpu.make_async_copy(gate, wgu.at[pl.ds(0, 384)], load_sem.at[2])
    w_up = pltpu.make_async_copy(up, wgu.at[pl.ds(384, 384)], load_sem.at[3])
    w_down = pltpu.make_async_copy(down, wd, load_sem.at[4])

    pending, final = [], []

    def send(like, to, name_here, name_there, source=None):
        ref = like()
        cp = pltpu.make_async_remote_copy(
            ref if source is None else source, ref, send_sem[name_here], recv_sem[name_there],
            device_id=to, device_id_type=MESH)
        cp.start()
        pending.append((name_here, like))

    def landed(ref, name):
        pltpu.make_async_remote_copy(
            ref, ref, send_sem[("x+", 0, "m", 0)], recv_sem[name], device_id=sib, device_id_type=MESH).wait_recv()

    def eighth(rel, s):
        q = 2 * (s // 2 % 2) + (par if rel == 0 else 1 - par)
        return pl.ds(pl.multiple_of(q * 1024 + s % 2 * 512, 512), 512)

    def piece(dz, dy, rel, s):
        zz = zh if dz == 0 else 1 - zh
        return xg.at[s // 4, zz, c, (y + dy) % 4, :, eighth(rel, s)]

    def group(dz, rel, s, cc):
        zz = zh if dz == 0 else 1 - zh
        q = 2 * (s % 2) + (par if rel == 0 else 1 - par)
        return xg.at[s // 2, zz, cc, :, :, pl.ds(pl.multiple_of(q * 1024, 1024), 1024)]

    DY = {"m": 3, "p": 1, "2": 2}

    def given(rel, s):
        return (tok, cot)[s // 4].at[:, eighth(rel, s)]

    def spread_y(dz, s):
        source = given(0, s) if dz == 0 else None
        send(lambda: piece(dz, 0, 0, s), yp, ("y+", dz, s), ("y", dz, "m", s), source)
        send(lambda: piece(dz, 0, 0, s), ym, ("y-", dz, s), ("y", dz, "p", s), source)

    def share_x(dz, who, s):
        forward = {"m": True, "p": False, "2": s % 2 == 0}[who]
        forward = forward if s < 4 else not forward
        send(lambda: piece(dz, DY[who], 0, s), xp if forward else xm, ("x+", dz, who, s), ("x", dz, who, s))

    def on_y(dz, who, s):
        landed(piece(dz, DY[who], 0, s), ("y", dz, who, s))
        if who == "m" and s % 2 == 0:
            send(lambda: piece(dz, DY[who], 0, s), yp, ("y2", dz, s), ("y", dz, "2", s))
        if who == "p" and s % 2 == 1:
            send(lambda: piece(dz, DY[who], 0, s), ym, ("y2", dz, s), ("y", dz, "2", s))
        share_x(dz, who, s)

    def on_x(dz, who, s):
        landed(piece(dz, DY[who], 1, s), ("x", dz, who, s))

    edge_pending = []

    def at_edge(like, to, name_here, name_there, source=None, arrived=None):
        edge_pending.append((name_here, like))

        @pl.when(edge)
        def _():
            if arrived is not None:
                landed(like(), arrived)
            pltpu.make_async_remote_copy(
                like() if source is None else source, like(), send_sem[name_here], recv_sem[name_there],
                device_id=to, device_id_type=MESH).start()

    def z_edge(rel, quarter):
        for s in (2 * quarter, 2 * quarter + 1):
            at_edge(lambda s=s: piece(1, 0, rel, s), inn, ("zi", rel, s), ("z", rel, s), arrived=("z", rel, s))

    def z_in(rel, s):
        pl.when(~edge)(lambda: landed(piece(1, 0, rel, s), ("z", rel, s)))

    def z_inner(rel, quarter):
        for s in (2 * quarter, 2 * quarter + 1):
            z_in(rel, s)

    def to_sibling(dz, rel, s):
        k = dz * 8 + rel * 4 + s
        cp = pltpu.make_async_remote_copy(
            group(dz, rel, s, c), group(dz, rel, s, c), out_sem.at[k], in_sem.at[k], device_id=sib, device_id_type=MESH)
        cp.start()

    def multiply(step):
        dz, rel, s = step // 8, step // 4 % 2, step % 4
        zz = jnp.where(dz == 0, zh, 1 - zh)
        q = 2 * (s % 2) + jnp.where(rel == 0, par, 1 - par)
        cols = pl.ds(pl.multiple_of(q * 1024, 1024), 1024)
        arrived = xg.at[s // 2, zz, 1 - c, :, :, cols]
        pltpu.make_async_remote_copy(
            arrived, arrived, out_sem.at[step], in_sem.at[step], device_id=sib, device_id_type=MESH).wait_recv()

        def add(arr, w, acc):
            rows = xg[arr, zz, :, :, :, cols].reshape(256, 1024)
            size = 256 if arr == 0 else 384
            for m in range(0, w.shape[0], size):
                at = pl.ds(m, size)
                acc[dz, at, :] += lax.dot_general(w[at, cols], rows, NT, preferred_element_type=jnp.float32)

        pl.when(s < 2)(lambda: add(0, wgu, accx))
        pl.when(s >= 2)(lambda: add(1, wd, accg))

    def lblock(dz, dy):
        return lmat.at[zh if dz == 0 else 1 - zh, c, (y + dy) % 4]

    def l_spread(dz):
        send(lambda: lblock(dz, 0), yp, ("ly+", dz), ("ly", dz, "m"))
        send(lambda: lblock(dz, 0), ym, ("ly-", dz), ("ly", dz, "p"))

    def l_on_y(dz):
        landed(lblock(dz, 3), ("ly", dz, "m"))
        send(lambda: lblock(dz, 3), yp, ("ly2", dz), ("ly", dz, "2"))
        landed(lblock(dz, 1), ("ly", dz, "p"))

    def lgroup(dz, cc):
        return lmat.at[zh if dz == 0 else 1 - zh, cc]

    def l_sibling(dz):
        landed(lblock(dz, 2), ("ly", dz, "2"))
        send(lambda: lgroup(dz, c), sib, ("lc", dz), ("lc", dz))

    def l_done(dz):
        landed(lgroup(dz, 1 - c), ("lc", dz))

    def greet(k):
        pl.semaphore_signal(met.at[2 * k], inc=1, device_id=zp, device_id_type=MESH)
        pl.semaphore_signal(met.at[2 * k + 1], inc=1, device_id=zm, device_id_type=MESH)

    def greeted(k):
        pl.semaphore_wait(met.at[2 * k], 1)
        pl.semaphore_wait(met.at[2 * k + 1], 1)

    def halves(quarter):
        return (2 * quarter, 2 * quarter + 1)

    def on_y_both(dz, quarter):
        for s in halves(quarter):
            on_y(dz, "m", s)
            on_y(dz, "p", s)

    def on_y2(dz, quarter):
        for s in halves(quarter):
            landed(piece(dz, 2, 0, s), ("y", dz, "2", s))
            share_x(dz, "2", s)
        to_sibling(dz, 0, quarter)

    def on_x_all(dz, quarter):
        for s in halves(quarter):
            on_x(dz, "m", s)
            on_x(dz, "p", s)
            on_x(dz, "2", s)
        to_sibling(dz, 1, quarter)

    def l_edge():
        at_edge(lambda: lblock(1, 0), inn, ("lzi",), ("lz",), arrived=("lz",))

    def l_on_z():
        pl.when(~edge)(lambda: landed(lblock(1, 0), ("lz",)))
        l_spread(1)

    def own(quarter):
        for s in halves(quarter):
            spread_y(0, s)
            at_edge(lambda s=s: piece(0, 0, 0, s), outn, ("zo", 0, s), ("z", 0, s), given(0, s))

    def own_rest(quarter):
        for s in halves(quarter):
            at_edge(lambda s=s: piece(0, 0, 1, s), outn, ("zo", 1, s), ("z", 1, s), given(1, s))

    def other(quarter):
        for s in halves(quarter):
            z_in(0, s)
            spread_y(1, s)

    half = lax.broadcasted_iota(jnp.int32, (8, 256), 0) < 4

    def over_experts(v, op):
        t = op(v, axis=0)
        a = op(t[0:4], axis=0, keepdims=True)
        b = op(t[4:8], axis=0, keepdims=True)
        return jnp.where(half, a, b)

    def softmax():
        l_done(0)
        l_done(1)
        for zz in range(2):
            flipped = lmat[zz].reshape(256, 128).T
            for k in range(16):
                probs[k, pl.ds(zz * 4, 4), :] = flipped[k * 4 : k * 4 + 4]
                chosen[k, pl.ds(zz * 4, 4), :] = flipped[64 + k * 4 : 68 + k * 4]
        raw = probs[...]
        raised = jnp.exp(raw - over_experts(raw, jnp.max))
        probs[...] = raised / over_experts(raised, jnp.sum)

    expert = lax.broadcasted_iota(jnp.int32, (64, 32), 0)
    picked = jnp.zeros((64, 32), jnp.float32)
    for k in range(8):
        picked += (routes[k : k + 1, :] == expert).astype(jnp.float32)
    lmat[zh, c, y, :, pl.ds(0, 64)] = logits[...]
    lmat[zh, c, y, :, pl.ds(64, 64)] = picked.T
    pl.semaphore_wait(barrier, 7)
    own(0)
    l_spread(0)
    at_edge(lambda: lblock(0, 0), outn, ("lzo",), ("lz",))
    for s in range(1, 4):
        own(s)
    for s in range(4):
        own_rest(s)
    for cp in (own_x, own_g, w_gate, w_up, w_down):
        cp.start()
    greet(0)
    accx[...] = jnp.zeros_like(accx)
    accg[...] = jnp.zeros_like(accg)
    own_x.wait()
    own_g.wait()
    on_y_both(0, 0)
    l_edge()
    z_edge(0, 0)
    on_y_both(0, 1)
    z_edge(0, 1)
    l_on_y(0)
    greeted(0)
    greet(1)
    on_y_both(0, 2)
    z_edge(0, 2)
    other(0)
    l_on_z()
    on_y_both(0, 3)
    z_edge(0, 3)
    other(1)
    on_y2(0, 0)
    greeted(1)
    greet(2)
    on_y2(0, 1)
    other(2)
    z_edge(1, 0)
    on_y_both(1, 0)
    on_y2(0, 2)
    other(3)
    z_edge(1, 1)
    w_gate.wait()
    w_up.wait()
    w_down.wait()

    def before_1():
        on_y_both(1, 1)
        on_y2(0, 3)
        z_edge(1, 2)
        l_sibling(0)
        on_x_all(0, 0)

    def before_2():
        on_y_both(1, 2)
        z_edge(1, 3)
        on_x_all(0, 1)

    def before_3():
        on_y_both(1, 3)
        on_x_all(0, 2)

    def before_4():
        on_y2(1, 0)

    def before_5():
        on_y2(1, 1)
        l_on_y(1)
        greeted(2)

    def before_6():
        on_x_all(0, 3)

    def before_7():
        on_y2(1, 2)

    def before_8():
        on_y2(1, 3)
        z_inner(1, 0)
        on_x_all(1, 0)

    def before_9():
        l_sibling(1)
        z_inner(1, 1)
        on_x_all(1, 1)

    def before_11():
        z_inner(1, 2)
        on_x_all(1, 2)

    def before_13():
        z_inner(1, 3)
        on_x_all(1, 3)

    before = {1: before_1, 2: before_2, 3: before_3, 4: before_4, 5: before_5, 6: before_6, 7: before_7, 8: before_8,
              9: before_9, 11: before_11, 13: before_13, 14: softmax}

    def at_step(step, low, high):
        if not any(low <= k < high for k in before):
            return
        if high - low == 1:
            before[low]()
            return
        mid = (low + high) // 2
        lax.cond(step < mid, lambda: at_step(step, low, mid), lambda: at_step(step, mid, high))

    @pl.loop(0, 16)
    def _(step):
        at_step(step, 0, 16)
        multiply(step)

    def local_scores(dz):
        g = accx[dz, 0:384, :]
        hidden = g / (1.0 + jnp.exp(-g)) * accx[dz, 384:768, :]
        both = hidden * accg[dz]
        return jnp.concatenate([jnp.sum(both[k * 96 : k * 96 + 96], axis=0, keepdims=True) for k in range(4)], axis=0)

    here, there = local_scores(0), local_scores(1)
    part[...] = jnp.where(zh == 0, jnp.concatenate([here, there], 0), jnp.concatenate([there, here], 0))

    def exchange(tag, source, place, peers):
        copies = {}
        for k, to in peers:
            copies[k] = pltpu.make_async_remote_copy(
                source, place(k), send_sem[(tag, k)], recv_sem[(tag, k)], device_id=to, device_id_type=MESH)
            copies[k].start()
        final.extend(copies.values())
        return copies

    copies = exchange("ty", part, lambda k: got_y.at[k], [
        (dy * 2 + dc, dev(x, (y + dy) % 4, z, (c + dc) % 2)) for dy, dc in ((2, 1), (2, 0), (1, 1), (3, 1), (1, 0), (3, 0), (0, 1))])
    for k in (1, 2, 6, 3, 7, 4, 5):
        copies[k].wait_recv()
    total[...] = part[...] + sum(got_y[k] for k in range(1, 8))
    copies = exchange("tz", total, lambda k: got_z.at[k], [(k, dev(x, y, (z + k) % 8, c)) for k in (4, 3, 5, 2, 6, 1, 7)])
    for k in (1, 7, 2, 6, 3, 5, 4):
        copies[k].wait_recv()
    for k in range(4):
        first = total[...] if k == 0 else got_z[k]
        got2[x * 4 + (z + 8 - k) % 4] = first + got_z[k + 4]
    mine = got2.at[pl.ds(x * 4, 4)]
    copies = exchange("tx", mine, lambda k: mine, [(k, dev((x + k) % 4, y, z, c)) for k in (2, 1, 3)])
    for k in (1, 3, 2):
        theirs = got2.at[pl.ds((x + 4 - k) % 4 * 4, 4)]
        pltpu.make_async_remote_copy(
            theirs, theirs, send_sem[("tx", k)], recv_sem[("tx", k)], device_id=sib, device_id_type=MESH).wait_recv()

    scores = got2[...]
    pr, ch = probs[...], chosen[...]
    kept = pr * ch
    mass = over_experts(kept, jnp.sum)
    weighted = over_experts(kept * scores, jnp.sum)
    prob_grad = scores / mass - ch * (weighted / (mass * mass))
    grad = pr * (prob_grad - over_experts(pr * prob_grad, jnp.sum))
    for k in range(16):
        lgc[0, pl.ds(k * 4, 4), :] = grad[k, 0:4]
        lgc[1, pl.ds(k * 4, 4), :] = grad[k, 4:8]
    turned[...] = lgc[zh].T
    lg_out[...] = turned[pl.ds(c * 128 + y * 32, 32), :]
    cols = pl.ds(pl.multiple_of(d * 256, 256), 256)
    rg = jnp.zeros((64, 256), jnp.float32)
    for zz in range(2):
        rows = xg[0, zz, :, :, :, cols].reshape(256, 256)
        rg += jnp.dot(lgc[zz].astype(jnp.bfloat16), rows, preferred_element_type=jnp.float32)
    rg_out[...] = rg

    def sent(name, like):
        pltpu.make_async_remote_copy(
            like(), like(), send_sem[name], recv_sem[("lz",)], device_id=sib, device_id_type=MESH).wait_send()

    for name, like in pending:
        sent(name, like)
    for step in range(16):
        ref = group(0, 0, 0, c)
        pltpu.make_async_remote_copy(
            ref, ref, out_sem.at[step], in_sem.at[step], device_id=sib, device_id_type=MESH).wait_send()
    for cp in final:
        cp.wait_send()

    @pl.when(edge)
    def _():
        for name, like in edge_pending:
            sent(name, like)


N_SEND, N_RECV = 160, 160


def finish(lg, rg, lg_out, rg_out):
    lg_out[...] = lg[...]
    rg_out[...] = rg[...]


def per_device(tokens, cotangent, logits, routes, gate_weight, up_weight, down_weight):
    flat = [w.reshape(384, 4096) for w in (gate_weight, up_weight, down_weight)]
    hbm, vmem = pl.BlockSpec(memory_space=pl.ANY), pl.BlockSpec(memory_space=pltpu.VMEM)
    f32, bf16 = jnp.float32, jnp.bfloat16
    logit_grad, router_grad = pl.pallas_call(
        kernel,
        out_shape=(jax.ShapeDtypeStruct((32, 64), f32), jax.ShapeDtypeStruct((64, 256), f32)),
        in_specs=[hbm, hbm, vmem, vmem, hbm, hbm, hbm],
        out_specs=(vmem, vmem),
        scratch_shapes=[
            pltpu.VMEM((2, 2, 2, 4, 32, 4096), bf16),
            pltpu.VMEM((768, 4096), bf16),
            pltpu.VMEM((384, 4096), bf16),
            pltpu.VMEM((2, 768, 256), f32),
            pltpu.VMEM((2, 384, 256), f32),
            pltpu.VMEM((2, 2, 4, 32, 128), f32),
            pltpu.VMEM((16, 8, 256), f32),
            pltpu.VMEM((16, 8, 256), f32),
            pltpu.VMEM((8, 256), f32),
            pltpu.VMEM((8, 256), f32),
            pltpu.VMEM((8, 8, 256), f32),
            pltpu.VMEM((8, 8, 256), f32),
            pltpu.VMEM((16, 8, 256), f32),
            pltpu.VMEM((2, 64, 256), f32),
            pltpu.VMEM((256, 64), f32),
            pltpu.SemaphoreType.DMA((5,)),
            pltpu.SemaphoreType.DMA((N_SEND,)),
            pltpu.SemaphoreType.DMA((N_RECV,)),
            pltpu.SemaphoreType.DMA((16,)),
            pltpu.SemaphoreType.DMA((16,)),
            pltpu.SemaphoreType.REGULAR((6,)),
        ],
        compiler_params=pltpu.CompilerParams(
            collective_id=0, has_side_effects=True, vmem_limit_bytes=60 * MIB),
        cost_estimate=pl.CostEstimate(flops=2 * 512 * 384 * 4096 * 3, bytes_accessed=10 * MIB, transcendentals=512 * 384),
        name="router_grad",
    )(tokens, cotangent, logits, routes.T, *flat)
    logit_grad, router_grad = pl.pallas_call(
        finish,
        out_shape=(jax.ShapeDtypeStruct((32, 64), f32), jax.ShapeDtypeStruct((64, 256), f32)),
        in_specs=[vmem, vmem],
        out_specs=(vmem, vmem),
        name="finish",
    )(logit_grad, router_grad)
    return logit_grad, router_grad.T


def solution(mesh):
    rows = P("dp", None)
    placed = (rows, rows, rows, rows) + (P("expert", "dp", None),) * 3
    return jax.shard_map(
        per_device, mesh=mesh, in_specs=placed, out_specs=(rows, rows), check_vma=False)
```

time: 56.1 us -> 54.9 us (0.979)
  local copies, waits for them, and re-layouts: 2.8 us -> 0 us
  Pallas kernels: 52.3 us -> 53.6 us
    unnamed x2 -> x0, local copies, waits for them, and re-layouts: 2.8 us -> none
    pallas_call x0 -> x1, Pallas kernels: none -> 1.5 us  [per_device(): pl.pallas_call(finish, out_shape=(jax.ShapeDtypeStruct((32, 64), f32), ja...]
where the time goes in v3:
time: 54.9 us; the launch traced here: 54.2 us
  Pallas kernels  53.6 us (98%)
  between operations  0.64 us (1%)
    pallas_call x1, Pallas kernels, per_device(): pl.pallas_call(kernel, out_shape=(jax.ShapeDtypeStruct((32, 64), f32), ja...  52.1 us
    pallas_call x1, Pallas kernels, per_device(): pl.pallas_call(finish, out_shape=(jax.ShapeDtypeStruct((32, 64), f32), ja...  1.5 us

profile of v3, /device:TPU:2, one launch (start us, length us, event | category | flops | bytes accessed | tf_op | source)
XLA Modules:
  0.0 54.2 jit_solution(7365758480850135129)
XLA Ops:
  0.6 52.1 %router_grad.1 = (f32[32,64]{1,0:T(8,128)}, f32[64,256]{1,0:T(8,128)}) custom-call(bf16[32,4096]{1,0:T(8,128)(2,1)} %tok.1, bf16[32,4096]{1,0:T(8,128)(2,1)} %cot.1, f32[32,64]{1,0:T(8,128)} %logits.1, s32[8,32]{1,0:T(8,128)} %bitcast.9, bf16[384,4096]{1,0:T(8,128)(2,1)} %bitcast.5, bf16[384,4096]{1,0:T(8,128)(2,1)} %bitcast.6, bf16[384,4096]{1,0:T(8,128)(2,1)} %bitcast.7), custom_call_target="tpu_custom_call" | custom-call | flops 4831838208 | bytes 10485760 | tf_op jit(solution)/shard_map/router_grad/pallas_call | solution.py:448
  52.7 1.5 %finish.1 = (f32[32,64]{1,0:T(8,128)}, f32[64,256]{1,0:T(8,128)}) custom-call(f32[32,64]{1,0:T(8,128)} %get-tuple-element.6.lg, f32[64,256]{1,0:T(8,128)} %get-tuple-element.7.rg), custom_call_target="tpu_custom_call" | custom-call | tf_op jit(solution)/shard_map/finish/pallas_call | solution.py:481

commit v4 on v3

--- a/solution.py
+++ b/solution.py
@@ -15,19 +15,21 @@
         self.ref, self.names = ref, {}
 
     def __getitem__(self, name):
-        return self.ref.at[self.names.setdefault(name, len(self.names))]
+        k = self.names.setdefault(name, len(self.names))
+        assert k < N_RECV
+        return self.ref.at[k]
 
 
 def kernel(tok, cot, logits, routes, gate, up, down, lg_out, rg_out,
            xg, wgu, wd, accx, accg, lmat, probs, chosen, part, total, got_y, got_z, got2, lgc, turned,
-           load_sem, send_ref, recv_ref, out_sem, in_sem, met):
+           load_sem, sent_sem, recv_ref, in_sem, met):
     d = lax.axis_index("dp")
     e = lax.axis_index("expert")
     y, zh, c = d // 4, (d // 2) % 2, d % 2
     x, zl = e // 4, e % 4
     z = zh * 4 + zl
     par = x % 2
-    send_sem, recv_sem = Sems(send_ref), Sems(recv_ref)
+    recv_sem = Sems(recv_ref)
 
     def dev(x_, y_, z_, c_):
         return ((y_ * 2 + z_ // 4) * 2 + c_, x_ * 4 + z_ % 4)
@@ -50,19 +52,19 @@
     w_up = pltpu.make_async_copy(up, wgu.at[pl.ds(384, 384)], load_sem.at[3])
     w_down = pltpu.make_async_copy(down, wd, load_sem.at[4])
 
-    pending, final = [], []
-
-    def send(like, to, name_here, name_there, source=None):
-        ref = like()
-        cp = pltpu.make_async_remote_copy(
-            ref if source is None else source, ref, send_sem[name_here], recv_sem[name_there],
-            device_id=to, device_id_type=MESH)
-        cp.start()
-        pending.append((name_here, like))
+
+    def send(ref, to, kind, name_there, source=None):
+        pltpu.make_async_remote_copy(
+            ref if source is None else source, ref, sent_sem.at[kind], recv_sem[name_there],
+            device_id=to, device_id_type=MESH).start()
 
     def landed(ref, name):
         pltpu.make_async_remote_copy(
-            ref, ref, send_sem[("x+", 0, "m", 0)], recv_sem[name], device_id=sib, device_id_type=MESH).wait_recv()
+            ref, ref, sent_sem.at[0], recv_sem[name], device_id=sib, device_id_type=MESH).wait_recv()
+
+    def sent(ref, kind):
+        pltpu.make_async_remote_copy(
+            ref, ref, sent_sem.at[kind], recv_sem[("lz",)], device_id=sib, device_id_type=MESH).wait_send()
 
     def eighth(rel, s):
         q = 2 * (s // 2 % 2) + (par if rel == 0 else 1 - par)
@@ -84,53 +86,53 @@
 
     def spread_y(dz, s):
         source = given(0, s) if dz == 0 else None
-        send(lambda: piece(dz, 0, 0, s), yp, ("y+", dz, s), ("y", dz, "m", s), source)
-        send(lambda: piece(dz, 0, 0, s), ym, ("y-", dz, s), ("y", dz, "p", s), source)
+        send(piece(dz, 0, 0, s), yp, 0, ("y", dz, "m", s), source)
+        send(piece(dz, 0, 0, s), ym, 0, ("y", dz, "p", s), source)
 
     def share_x(dz, who, s):
         forward = {"m": True, "p": False, "2": s % 2 == 0}[who]
         forward = forward if s < 4 else not forward
-        send(lambda: piece(dz, DY[who], 0, s), xp if forward else xm, ("x+", dz, who, s), ("x", dz, who, s))
+        send(piece(dz, DY[who], 0, s), xp if forward else xm, 0, ("x", dz, s // 2))
 
     def on_y(dz, who, s):
         landed(piece(dz, DY[who], 0, s), ("y", dz, who, s))
         if who == "m" and s % 2 == 0:
-            send(lambda: piece(dz, DY[who], 0, s), yp, ("y2", dz, s), ("y", dz, "2", s))
+            send(piece(dz, DY[who], 0, s), yp, 0, ("y", dz, "2", s))
         if who == "p" and s % 2 == 1:
-            send(lambda: piece(dz, DY[who], 0, s), ym, ("y2", dz, s), ("y", dz, "2", s))
+            send(piece(dz, DY[who], 0, s), ym, 0, ("y", dz, "2", s))
         share_x(dz, who, s)
 
-    def on_x(dz, who, s):
-        landed(piece(dz, DY[who], 1, s), ("x", dz, who, s))
-
-    edge_pending = []
-
-    def at_edge(like, to, name_here, name_there, source=None, arrived=None):
-        edge_pending.append((name_here, like))
-
+    def at_edge(like, to, kind, name_there, source=None, arrived=None):
         @pl.when(edge)
         def _():
             if arrived is not None:
                 landed(like(), arrived)
-            pltpu.make_async_remote_copy(
-                like() if source is None else source, like(), send_sem[name_here], recv_sem[name_there],
-                device_id=to, device_id_type=MESH).start()
+            send(like(), to, kind, name_there, source)
+
+    def quarter_of(rel, quarter):
+        q = 2 * (quarter % 2) + (par if rel == 0 else 1 - par)
+        return pl.ds(pl.multiple_of(q * 1024, 1024), 1024)
+
+    def other_own(quarter):
+        return xg.at[quarter // 2, 1 - zh, c, y, :, quarter_of(1, quarter)]
 
     def z_edge(rel, quarter):
+        if rel == 1:
+            at_edge(lambda: other_own(quarter), inn, 2, ("z1", quarter), arrived=("z1", quarter))
+            return
         for s in (2 * quarter, 2 * quarter + 1):
-            at_edge(lambda s=s: piece(1, 0, rel, s), inn, ("zi", rel, s), ("z", rel, s), arrived=("z", rel, s))
-
-    def z_in(rel, s):
-        pl.when(~edge)(lambda: landed(piece(1, 0, rel, s), ("z", rel, s)))
-
-    def z_inner(rel, quarter):
-        for s in (2 * quarter, 2 * quarter + 1):
-            z_in(rel, s)
+            at_edge(lambda s=s: piece(1, 0, 0, s), inn, 2, ("z", s), arrived=("z", s))
+
+    def z_in(s):
+        pl.when(~edge)(lambda: landed(piece(1, 0, 0, s), ("z", s)))
+
+    def z_inner(quarter):
+        pl.when(~edge)(lambda: landed(other_own(quarter), ("z1", quarter)))
 
     def to_sibling(dz, rel, s):
         k = dz * 8 + rel * 4 + s
         cp = pltpu.make_async_remote_copy(
-            group(dz, rel, s, c), group(dz, rel, s, c), out_sem.at[k], in_sem.at[k], device_id=sib, device_id_type=MESH)
+            group(dz, rel, s, c), group(dz, rel, s, c), sent_sem.at[1], in_sem.at[k], device_id=sib, device_id_type=MESH)
         cp.start()
 
     def multiply(step):
@@ -140,7 +142,7 @@
         cols = pl.ds(pl.multiple_of(q * 1024, 1024), 1024)
         arrived = xg.at[s // 2, zz, 1 - c, :, :, cols]
         pltpu.make_async_remote_copy(
-            arrived, arrived, out_sem.at[step], in_sem.at[step], device_id=sib, device_id_type=MESH).wait_recv()
+            arrived, arrived, sent_sem.at[1], in_sem.at[step], device_id=sib, device_id_type=MESH).wait_recv()
 
         def add(arr, w, acc):
             rows = xg[arr, zz, :, :, :, cols].reshape(256, 1024)
@@ -156,12 +158,12 @@
         return lmat.at[zh if dz == 0 else 1 - zh, c, (y + dy) % 4]
 
     def l_spread(dz):
-        send(lambda: lblock(dz, 0), yp, ("ly+", dz), ("ly", dz, "m"))
-        send(lambda: lblock(dz, 0), ym, ("ly-", dz), ("ly", dz, "p"))
+        send(lblock(dz, 0), yp, 3, ("ly", dz, "m"))
+        send(lblock(dz, 0), ym, 3, ("ly", dz, "p"))
 
     def l_on_y(dz):
         landed(lblock(dz, 3), ("ly", dz, "m"))
-        send(lambda: lblock(dz, 3), yp, ("ly2", dz), ("ly", dz, "2"))
+        send(lblock(dz, 3), yp, 3, ("ly", dz, "2"))
         landed(lblock(dz, 1), ("ly", dz, "p"))
 
     def lgroup(dz, cc):
@@ -169,7 +171,7 @@
 
     def l_sibling(dz):
         landed(lblock(dz, 2), ("ly", dz, "2"))
-        send(lambda: lgroup(dz, c), sib, ("lc", dz), ("lc", dz))
+        send(lgroup(dz, c), sib, 4, ("lc", dz))
 
     def l_done(dz):
         landed(lgroup(dz, 1 - c), ("lc", dz))
@@ -197,14 +199,11 @@
         to_sibling(dz, 0, quarter)
 
     def on_x_all(dz, quarter):
-        for s in halves(quarter):
-            on_x(dz, "m", s)
-            on_x(dz, "p", s)
-            on_x(dz, "2", s)
+        landed(xg.at[0, 0, 0, pl.ds(0, 3), :, pl.ds(0, 1024)], ("x", dz, quarter))
         to_sibling(dz, 1, quarter)
 
     def l_edge():
-        at_edge(lambda: lblock(1, 0), inn, ("lzi",), ("lz",), arrived=("lz",))
+        at_edge(lambda: lblock(1, 0), inn, 5, ("lz",), arrived=("lz",))
 
     def l_on_z():
         pl.when(~edge)(lambda: landed(lblock(1, 0), ("lz",)))
@@ -213,15 +212,15 @@
     def own(quarter):
         for s in halves(quarter):
             spread_y(0, s)
-            at_edge(lambda s=s: piece(0, 0, 0, s), outn, ("zo", 0, s), ("z", 0, s), given(0, s))
+            at_edge(lambda s=s: piece(0, 0, 0, s), outn, 2, ("z", s), given(0, s))
 
     def own_rest(quarter):
-        for s in halves(quarter):
-            at_edge(lambda s=s: piece(0, 0, 1, s), outn, ("zo", 1, s), ("z", 1, s), given(1, s))
+        cols = quarter_of(1, quarter)
+        at_edge(lambda: xg.at[quarter // 2, zh, c, y, :, cols], outn, 2, ("z1", quarter), (tok, cot)[quarter // 2].at[:, cols])
 
     def other(quarter):
         for s in halves(quarter):
-            z_in(0, s)
+            z_in(s)
             spread_y(1, s)
 
     half = lax.broadcasted_iota(jnp.int32, (8, 256), 0) < 4
@@ -253,7 +252,7 @@
     pl.semaphore_wait(barrier, 7)
     own(0)
     l_spread(0)
-    at_edge(lambda: lblock(0, 0), outn, ("lzo",), ("lz",))
+    at_edge(lambda: lblock(0, 0), outn, 5, ("lz",))
     for s in range(1, 4):
         own(s)
     for s in range(4):
@@ -302,48 +301,47 @@
         on_x_all(0, 0)
 
     def before_2():
-        on_y_both(1, 2)
         z_edge(1, 3)
         on_x_all(0, 1)
 
     def before_3():
+        on_y_both(1, 2)
+        on_x_all(0, 2)
+        l_on_y(1)
+
+    def before_5():
         on_y_both(1, 3)
-        on_x_all(0, 2)
-
-    def before_4():
         on_y2(1, 0)
-
-    def before_5():
+        on_x_all(0, 3)
+
+    def before_6():
         on_y2(1, 1)
-        l_on_y(1)
         greeted(2)
-
-    def before_6():
-        on_x_all(0, 3)
-
-    def before_7():
+        l_sibling(1)
+
+    def before_8():
         on_y2(1, 2)
 
-    def before_8():
+    def before_10():
         on_y2(1, 3)
-        z_inner(1, 0)
+        z_inner(0)
         on_x_all(1, 0)
-
-    def before_9():
-        l_sibling(1)
-        z_inner(1, 1)
+        softmax()
+
+    def before_11():
+        z_inner(1)
         on_x_all(1, 1)
 
-    def before_11():
-        z_inner(1, 2)
+    def before_12():
+        z_inner(2)
         on_x_all(1, 2)
 
     def before_13():
-        z_inner(1, 3)
+        z_inner(3)
         on_x_all(1, 3)
 
-    before = {1: before_1, 2: before_2, 3: before_3, 4: before_4, 5: before_5, 6: before_6, 7: before_7, 8: before_8,
-              9: before_9, 11: before_11, 13: before_13, 14: softmax}
+    before = {1: before_1, 2: before_2, 3: before_3, 5: before_5, 6: before_6, 8: before_8,
+              10: before_10, 11: before_11, 12: before_12, 13: before_13}
 
     def at_step(step, low, high):
         if not any(low <= k < high for k in before):
@@ -357,7 +355,7 @@
     @pl.loop(0, 16)
     def _(step):
         at_step(step, 0, 16)
-        multiply(step)
+        multiply(jnp.where(step == 11, 12, jnp.where(step == 12, 11, step)))
 
     def local_scores(dz):
         g = accx[dz, 0:384, :]
@@ -368,32 +366,23 @@
     here, there = local_scores(0), local_scores(1)
     part[...] = jnp.where(zh == 0, jnp.concatenate([here, there], 0), jnp.concatenate([there, here], 0))
 
-    def exchange(tag, source, place, peers):
-        copies = {}
+    def exchange(kind, source, place, peers):
         for k, to in peers:
-            copies[k] = pltpu.make_async_remote_copy(
-                source, place(k), send_sem[(tag, k)], recv_sem[(tag, k)], device_id=to, device_id_type=MESH)
-            copies[k].start()
-        final.extend(copies.values())
-        return copies
-
-    copies = exchange("ty", part, lambda k: got_y.at[k], [
+            pltpu.make_async_remote_copy(
+                source, place(k), sent_sem.at[kind], recv_sem[("t", kind)], device_id=to, device_id_type=MESH).start()
+
+    exchange(6, part, lambda k: got_y.at[k], [
         (dy * 2 + dc, dev(x, (y + dy) % 4, z, (c + dc) % 2)) for dy, dc in ((2, 1), (2, 0), (1, 1), (3, 1), (1, 0), (3, 0), (0, 1))])
-    for k in (1, 2, 6, 3, 7, 4, 5):
-        copies[k].wait_recv()
+    landed(got_y.at[pl.ds(1, 7)], ("t", 6))
     total[...] = part[...] + sum(got_y[k] for k in range(1, 8))
-    copies = exchange("tz", total, lambda k: got_z.at[k], [(k, dev(x, y, (z + k) % 8, c)) for k in (4, 3, 5, 2, 6, 1, 7)])
-    for k in (1, 7, 2, 6, 3, 5, 4):
-        copies[k].wait_recv()
+    exchange(7, total, lambda k: got_z.at[k], [(k, dev(x, y, (z + k) % 8, c)) for k in (4, 3, 5, 2, 6, 1, 7)])
+    landed(got_z.at[pl.ds(1, 7)], ("t", 7))
     for k in range(4):
         first = total[...] if k == 0 else got_z[k]
         got2[x * 4 + (z + 8 - k) % 4] = first + got_z[k + 4]
     mine = got2.at[pl.ds(x * 4, 4)]
-    copies = exchange("tx", mine, lambda k: mine, [(k, dev((x + k) % 4, y, z, c)) for k in (2, 1, 3)])
-    for k in (1, 3, 2):
-        theirs = got2.at[pl.ds((x + 4 - k) % 4 * 4, 4)]
-        pltpu.make_async_remote_copy(
-            theirs, theirs, send_sem[("tx", k)], recv_sem[("tx", k)], device_id=sib, device_id_type=MESH).wait_recv()
+    exchange(8, mine, lambda k: mine, [(k, dev((x + k) % 4, y, z, c)) for k in (2, 1, 3)])
+    landed(got2.at[pl.ds(0, 12)], ("t", 8))
 
     scores = got2[...]
     pr, ch = probs[...], chosen[...]
@@ -414,26 +403,21 @@
         rg += jnp.dot(lgc[zz].astype(jnp.bfloat16), rows, preferred_element_type=jnp.float32)
     rg_out[...] = rg
 
-    def sent(name, like):
-        pltpu.make_async_remote_copy(
-            like(), like(), send_sem[name], recv_sem[("lz",)], device_id=sib, device_id_type=MESH).wait_send()
-
-    for name, like in pending:
-        sent(name, like)
-    for step in range(16):
-        ref = group(0, 0, 0, c)
-        pltpu.make_async_remote_copy(
-            ref, ref, out_sem.at[step], in_sem.at[step], device_id=sib, device_id_type=MESH).wait_send()
-    for cp in final:
-        cp.wait_send()
+    sent(wd, 0)
+    sent(xg.at[0], 1)
+    sent(got2.at[pl.ds(0, 12)], 3)
+    sent(got2, 4)
+    sent(got_y.at[pl.ds(1, 7)], 6)
+    sent(got_z.at[pl.ds(1, 7)], 7)
+    sent(got2.at[pl.ds(0, 12)], 8)
 
     @pl.when(edge)
     def _():
-        for name, like in edge_pending:
-            sent(name, like)
-
-
-N_SEND, N_RECV = 160, 160
+        sent(xg.at[0, 0, 0], 2)
+        sent(got2.at[pl.ds(0, 4)], 5)
+
+
+N_RECV = 80
 
 
 def finish(lg, rg, lg_out, rg_out):
@@ -467,9 +451,8 @@
             pltpu.VMEM((2, 64, 256), f32),
             pltpu.VMEM((256, 64), f32),
             pltpu.SemaphoreType.DMA((5,)),
-            pltpu.SemaphoreType.DMA((N_SEND,)),
+            pltpu.SemaphoreType.DMA((9,)),
             pltpu.SemaphoreType.DMA((N_RECV,)),
-            pltpu.SemaphoreType.DMA((16,)),
             pltpu.SemaphoreType.DMA((16,)),
             pltpu.SemaphoreType.REGULAR((6,)),
         ],

time: 54.9 us -> 52.2 us (0.951)
  Pallas kernels: 53.6 us -> 51.2 us
    pallas_call x1, Pallas kernels: 52.1 us -> 49.7 us  [per_device(): pl.pallas_call(kernel, out_shape=(jax.ShapeDtypeStruct((32, 64), f32), ja...]
where the time goes in v4:
time: 52.2 us; the launch traced here: 51.8 us
  Pallas kernels  51.2 us (98%)
  between operations  0.64 us (1%)
    pallas_call x1, Pallas kernels, per_device(): pl.pallas_call(kernel, out_shape=(jax.ShapeDtypeStruct((32, 64), f32), ja...  49.7 us
    pallas_call x1, Pallas kernels, per_device(): pl.pallas_call(finish, out_shape=(jax.ShapeDtypeStruct((32, 64), f32), ja...  1.5 us

profile of v4, /device:TPU:2, one launch (start us, length us, event | category | flops | bytes accessed | tf_op | source)
XLA Modules:
  0.0 51.8 jit_solution(11486150815587553059)
XLA Ops:
  0.6 49.7 %router_grad.1 = (f32[32,64]{1,0:T(8,128)}, f32[64,256]{1,0:T(8,128)}) custom-call(bf16[32,4096]{1,0:T(8,128)(2,1)} %tok.1, bf16[32,4096]{1,0:T(8,128)(2,1)} %cot.1, f32[32,64]{1,0:T(8,128)} %logits.1, s32[8,32]{1,0:T(8,128)} %bitcast.9, bf16[384,4096]{1,0:T(8,128)(2,1)} %bitcast.5, bf16[384,4096]{1,0:T(8,128)(2,1)} %bitcast.6, bf16[384,4096]{1,0:T(8,128)(2,1)} %bitcast.7), custom_call_target="tpu_custom_call" | custom-call | flops 4831838208 | bytes 10485760 | tf_op jit(solution)/shard_map/router_grad/pallas_call | solution.py:432
  50.3 1.5 %finish.1 = (f32[32,64]{1,0:T(8,128)}, f32[64,256]{1,0:T(8,128)}) custom-call(f32[32,64]{1,0:T(8,128)} %get-tuple-element.6.lg, f32[64,256]{1,0:T(8,128)} %get-tuple-element.7.rg), custom_call_target="tpu_custom_call" | custom-call | tf_op jit(solution)/shard_map/finish/pallas_call | solution.py:464

commit v5 on v4

--- a/solution.py
+++ b/solution.py
@@ -243,42 +243,43 @@
         raised = jnp.exp(raw - over_experts(raw, jnp.max))
         probs[...] = raised / over_experts(raised, jnp.sum)
 
+    pl.semaphore_wait(barrier, 7)
+    own(0)
+    own(1)
+    for cp in (own_x, own_g, w_gate, w_up, w_down):
+        cp.start()
     expert = lax.broadcasted_iota(jnp.int32, (64, 32), 0)
     picked = jnp.zeros((64, 32), jnp.float32)
     for k in range(8):
         picked += (routes[k : k + 1, :] == expert).astype(jnp.float32)
     lmat[zh, c, y, :, pl.ds(0, 64)] = logits[...]
     lmat[zh, c, y, :, pl.ds(64, 64)] = picked.T
-    pl.semaphore_wait(barrier, 7)
-    own(0)
     l_spread(0)
     at_edge(lambda: lblock(0, 0), outn, 5, ("lz",))
-    for s in range(1, 4):
-        own(s)
+    own(2)
+    own(3)
     for s in range(4):
         own_rest(s)
-    for cp in (own_x, own_g, w_gate, w_up, w_down):
-        cp.start()
     greet(0)
     accx[...] = jnp.zeros_like(accx)
     accg[...] = jnp.zeros_like(accg)
     own_x.wait()
     own_g.wait()
     on_y_both(0, 0)
-    l_edge()
     z_edge(0, 0)
     on_y_both(0, 1)
     z_edge(0, 1)
-    l_on_y(0)
+    l_edge()
     greeted(0)
     greet(1)
     on_y_both(0, 2)
     z_edge(0, 2)
+    l_on_y(0)
     other(0)
-    l_on_z()
     on_y_both(0, 3)
     z_edge(0, 3)
     other(1)
+    l_on_z()
     on_y2(0, 0)
     greeted(1)
     greet(2)
@@ -431,7 +432,7 @@
     f32, bf16 = jnp.float32, jnp.bfloat16
     logit_grad, router_grad = pl.pallas_call(
         kernel,
-        out_shape=(jax.ShapeDtypeStruct((32, 64), f32), jax.ShapeDtypeStruct((64, 256), f32)),
+        out_shape=(pltpu.VMEM((32, 64), f32), pltpu.VMEM((64, 256), f32)),
         in_specs=[hbm, hbm, vmem, vmem, hbm, hbm, hbm],
         out_specs=(vmem, vmem),
         scratch_shapes=[
@@ -467,7 +468,7 @@
         in_specs=[vmem, vmem],
         out_specs=(vmem, vmem),
         name="finish",
-    )(logit_grad, router_grad)
+    )(*(pltpu.with_memory_space_constraint(v, pltpu.VMEM) for v in (logit_grad, router_grad)))
     return logit_grad, router_grad.T
 
 

time: 52.2 us -> 50.5 us (0.967)
  Pallas kernels: 51.2 us -> 49.6 us
    pallas_call x1, Pallas kernels: 1.5 us -> 0.64 us  [per_device(): pl.pallas_call(finish, out_shape=(jax.ShapeDtypeStruct((32, 64), f32), ja...]
    pallas_call x1, Pallas kernels: 49.7 us -> 49 us  [per_device(): pl.pallas_call(kernel, out_shape=(pltpu.VMEM((32, 64), f32), pltpu.VMEM((...]
where the time goes in v5:
time: 50.5 us; the launch traced here: 50.3 us
  Pallas kernels  49.6 us (98%)
  between operations  0.64 us (1%)
    pallas_call x1, Pallas kernels, per_device(): pl.pallas_call(kernel, out_shape=(pltpu.VMEM((32, 64), f32), pltpu.VMEM((...  49 us

profile of v5, /device:TPU:2, one launch (start us, length us, event | category | flops | bytes accessed | tf_op | source)
XLA Modules:
  0.0 50.3 jit_solution(9896895416233270420)
XLA Ops:
  0.6 49.0 %router_grad.1 = (f32[32,64]{1,0:T(8,128)S(1)}, f32[64,256]{1,0:T(8,128)S(1)}) custom-call(bf16[32,4096]{1,0:T(8,128)(2,1)} %tok.1, bf16[32,4096]{1,0:T(8,128)(2,1)} %cot.1, f32[32,64]{1,0:T(8,128)} %logits.1, s32[8,32]{1,0:T(8,128)} %bitcast.9, bf16[384,4096]{1,0:T(8,128)(2,1)} %bitcast.5, bf16[384,4096]{1,0:T(8,128)(2,1)} %bitcast.6, bf16[384,4096]{1,0:T(8,128)(2,1)} %bitcast.7), custom_call_target="tpu_custom_call" | custom-call | flops 4831838208 | bytes 10485760 | tf_op jit(solution)/shard_map/router_grad/pallas_call | solution.py:433
  49.6 0.6 %finish.1 = (f32[32,64]{1,0:T(8,128)}, f32[64,256]{1,0:T(8,128)}) custom-call(f32[32,64]{1,0:T(8,128)S(1)} %get-tuple-element.6.lg, f32[64,256]{1,0:T(8,128)S(1)} %get-tuple-element.7.rg), custom_call_target="tpu_custom_call" | custom-call | tf_op jit(solution)/shard_map/finish/pallas_call | solution.py:465

commit v6 on v5

--- a/solution.py
+++ b/solution.py
@@ -21,7 +21,7 @@
 
 
 def kernel(tok, cot, logits, routes, gate, up, down, lg_out, rg_out,
-           xg, wgu, wd, accx, accg, lmat, probs, chosen, part, total, got_y, got_z, got2, lgc, turned,
+           xg, wgu, wd, accx, accg, lmat, probs, chosen, early, part, total, got_y, got_z, got2, lgc, turned,
            load_sem, sent_sem, recv_ref, in_sem, met):
     d = lax.axis_index("dp")
     e = lax.axis_index("expert")
@@ -86,21 +86,20 @@
 
     def spread_y(dz, s):
         source = given(0, s) if dz == 0 else None
-        send(piece(dz, 0, 0, s), yp, 0, ("y", dz, "m", s), source)
-        send(piece(dz, 0, 0, s), ym, 0, ("y", dz, "p", s), source)
+        send(piece(dz, 0, 0, s), yp, 0, ("y", dz, s), source)
+        send(piece(dz, 0, 0, s), ym, 0, ("y", dz, s), source)
 
     def share_x(dz, who, s):
         forward = {"m": True, "p": False, "2": s % 2 == 0}[who]
         forward = forward if s < 4 else not forward
-        send(piece(dz, DY[who], 0, s), xp if forward else xm, 0, ("x", dz, s // 2))
-
-    def on_y(dz, who, s):
-        landed(piece(dz, DY[who], 0, s), ("y", dz, who, s))
-        if who == "m" and s % 2 == 0:
-            send(piece(dz, DY[who], 0, s), yp, 0, ("y", dz, "2", s))
-        if who == "p" and s % 2 == 1:
-            send(piece(dz, DY[who], 0, s), ym, 0, ("y", dz, "2", s))
-        share_x(dz, who, s)
+        send(piece(dz, DY[who], 0, s), xp if forward else xm, 0, ("x", dz, s // 2 if (dz, s) != (1, 7) else 4))
+
+    def on_y(dz, s):
+        landed(xg.at[0, 0, 0, 0, :, pl.ds(0, 1024)], ("y", dz, s))
+        who, to = ("m", yp) if s % 2 == 0 else ("p", ym)
+        send(piece(dz, DY[who], 0, s), to, 0, ("y2", dz, s // 2))
+        share_x(dz, "m", s)
+        share_x(dz, "p", s)
 
     def at_edge(like, to, kind, name_there, source=None, arrived=None):
         @pl.when(edge)
@@ -158,47 +157,51 @@
         return lmat.at[zh if dz == 0 else 1 - zh, c, (y + dy) % 4]
 
     def l_spread(dz):
-        send(lblock(dz, 0), yp, 3, ("ly", dz, "m"))
-        send(lblock(dz, 0), ym, 3, ("ly", dz, "p"))
+        send(lblock(dz, 0), yp, 3, ("ly", dz))
+        send(lblock(dz, 0), ym, 3, ("ly", dz))
 
     def l_on_y(dz):
-        landed(lblock(dz, 3), ("ly", dz, "m"))
-        send(lblock(dz, 3), yp, 3, ("ly", dz, "2"))
-        landed(lblock(dz, 1), ("ly", dz, "p"))
+        landed(lmat.at[0, 0, pl.ds(0, 2)], ("ly", dz))
+        send(lblock(dz, 3), yp, 3, ("ly2", dz))
 
     def lgroup(dz, cc):
         return lmat.at[zh if dz == 0 else 1 - zh, cc]
 
     def l_sibling(dz):
-        landed(lblock(dz, 2), ("ly", dz, "2"))
+        landed(lblock(dz, 2), ("ly2", dz))
         send(lgroup(dz, c), sib, 4, ("lc", dz))
 
     def l_done(dz):
         landed(lgroup(dz, 1 - c), ("lc", dz))
 
     def greet(k):
-        pl.semaphore_signal(met.at[2 * k], inc=1, device_id=zp, device_id_type=MESH)
-        pl.semaphore_signal(met.at[2 * k + 1], inc=1, device_id=zm, device_id_type=MESH)
+        pl.semaphore_signal(met.at[k], inc=1, device_id=zp, device_id_type=MESH)
+        pl.semaphore_signal(met.at[k], inc=1, device_id=zm, device_id_type=MESH)
 
     def greeted(k):
-        pl.semaphore_wait(met.at[2 * k], 1)
-        pl.semaphore_wait(met.at[2 * k + 1], 1)
+        pl.semaphore_wait(met.at[k], 2)
 
     def halves(quarter):
         return (2 * quarter, 2 * quarter + 1)
 
     def on_y_both(dz, quarter):
         for s in halves(quarter):
-            on_y(dz, "m", s)
-            on_y(dz, "p", s)
+            on_y(dz, s)
 
     def on_y2(dz, quarter):
+        landed(xg.at[0, 0, 0, 0, :, pl.ds(0, 1024)], ("y2", dz, quarter))
         for s in halves(quarter):
-            landed(piece(dz, 2, 0, s), ("y", dz, "2", s))
             share_x(dz, "2", s)
         to_sibling(dz, 0, quarter)
 
     def on_x_all(dz, quarter):
+        if (dz, quarter) == (1, 3):
+            for s in halves(3):
+                landed(xg.at[0, 0, 0, pl.ds(0, 3), :, pl.ds(0, 512)], ("x", 1, s - 3))
+                ref = xg.at[1, 1 - zh, c, :, :, eighth(1, s)]
+                pltpu.make_async_remote_copy(
+                    ref, ref, sent_sem.at[1], in_sem.at[15], device_id=sib, device_id_type=MESH).start()
+            return
         landed(xg.at[0, 0, 0, pl.ds(0, 3), :, pl.ds(0, 1024)], ("x", dz, quarter))
         to_sibling(dz, 1, quarter)
 
@@ -230,6 +233,12 @@
         a = op(t[0:4], axis=0, keepdims=True)
         b = op(t[4:8], axis=0, keepdims=True)
         return jnp.where(half, a, b)
+
+    def local_scores(dz):
+        g = accx[dz, 0:384, :]
+        hidden = g / (1.0 + jnp.exp(-g)) * accx[dz, 384:768, :]
+        both = hidden * accg[dz]
+        return jnp.concatenate([jnp.sum(both[k * 96 : k * 96 + 96], axis=0, keepdims=True) for k in range(4)], axis=0)
 
     def softmax():
         l_done(0)
@@ -328,6 +337,7 @@
         z_inner(0)
         on_x_all(1, 0)
         softmax()
+        early[...] = local_scores(0)
 
     def before_11():
         z_inner(1)
@@ -358,13 +368,7 @@
         at_step(step, 0, 16)
         multiply(jnp.where(step == 11, 12, jnp.where(step == 12, 11, step)))
 
-    def local_scores(dz):
-        g = accx[dz, 0:384, :]
-        hidden = g / (1.0 + jnp.exp(-g)) * accx[dz, 384:768, :]
-        both = hidden * accg[dz]
-        return jnp.concatenate([jnp.sum(both[k * 96 : k * 96 + 96], axis=0, keepdims=True) for k in range(4)], axis=0)
-
-    here, there = local_scores(0), local_scores(1)
+    here, there = early[...], local_scores(1)
     part[...] = jnp.where(zh == 0, jnp.concatenate([here, there], 0), jnp.concatenate([there, here], 0))
 
     def exchange(kind, source, place, peers):
@@ -418,7 +422,7 @@
         sent(got2.at[pl.ds(0, 4)], 5)
 
 
-N_RECV = 80
+N_RECV = 55
 
 
 def finish(lg, rg, lg_out, rg_out):
@@ -444,6 +448,7 @@
             pltpu.VMEM((2, 2, 4, 32, 128), f32),
             pltpu.VMEM((16, 8, 256), f32),
             pltpu.VMEM((16, 8, 256), f32),
+            pltpu.VMEM((4, 256), f32),
             pltpu.VMEM((8, 256), f32),
             pltpu.VMEM((8, 256), f32),
             pltpu.VMEM((8, 8, 256), f32),
@@ -455,7 +460,7 @@
             pltpu.SemaphoreType.DMA((9,)),
             pltpu.SemaphoreType.DMA((N_RECV,)),
             pltpu.SemaphoreType.DMA((16,)),
-            pltpu.SemaphoreType.REGULAR((6,)),
+            pltpu.SemaphoreType.REGULAR((3,)),
         ],
         compiler_params=pltpu.CompilerParams(
             collective_id=0, has_side_effects=True, vmem_limit_bytes=60 * MIB),

time: 50.5 us -> 50.6 us (level)
  no operation moved by 1% of the time
where the time goes in v6:
time: 50.6 us; the launch traced here: 50.4 us
  Pallas kernels  49.8 us (98%)
  between operations  0.64 us (1%)
    pallas_call x1, Pallas kernels, per_device(): pl.pallas_call(kernel, out_shape=(pltpu.VMEM((32, 64), f32), pltpu.VMEM((...  49.1 us

profile of v6, /device:TPU:2, one launch (start us, length us, event | category | flops | bytes accessed | tf_op | source)
XLA Modules:
  0.0 50.4 jit_solution(6397083872257463964)
XLA Ops:
  0.6 49.1 %router_grad.1 = (f32[32,64]{1,0:T(8,128)S(1)}, f32[64,256]{1,0:T(8,128)S(1)}) custom-call(bf16[32,4096]{1,0:T(8,128)(2,1)} %tok.1, bf16[32,4096]{1,0:T(8,128)(2,1)} %cot.1, f32[32,64]{1,0:T(8,128)} %logits.1, s32[8,32]{1,0:T(8,128)} %bitcast.9, bf16[384,4096]{1,0:T(8,128)(2,1)} %bitcast.5, bf16[384,4096]{1,0:T(8,128)(2,1)} %bitcast.6, bf16[384,4096]{1,0:T(8,128)(2,1)} %bitcast.7), custom_call_target="tpu_custom_call" | custom-call | flops 4831838208 | bytes 10485760 | tf_op jit(solution)/shard_map/router_grad/pallas_call | solution.py:437
  49.8 0.6 %finish.1 = (f32[32,64]{1,0:T(8,128)}, f32[64,256]{1,0:T(8,128)}) custom-call(f32[32,64]{1,0:T(8,128)S(1)} %get-tuple-element.6.lg, f32[64,256]{1,0:T(8,128)S(1)} %get-tuple-element.7.rg), custom_call_target="tpu_custom_call" | custom-call | tf_op jit(solution)/shard_map/finish/pallas_call | solution.py:470

commit v7 on v6

--- a/solution.py
+++ b/solution.py
@@ -380,13 +380,17 @@
         (dy * 2 + dc, dev(x, (y + dy) % 4, z, (c + dc) % 2)) for dy, dc in ((2, 1), (2, 0), (1, 1), (3, 1), (1, 0), (3, 0), (0, 1))])
     landed(got_y.at[pl.ds(1, 7)], ("t", 6))
     total[...] = part[...] + sum(got_y[k] for k in range(1, 8))
-    exchange(7, total, lambda k: got_z.at[k], [(k, dev(x, y, (z + k) % 8, c)) for k in (4, 3, 5, 2, 6, 1, 7)])
-    landed(got_z.at[pl.ds(1, 7)], ("t", 7))
-    for k in range(4):
+    for k in (4, 2, 6, 3, 5, 1, 7):
+        pltpu.make_async_remote_copy(
+            total, got_z.at[k], sent_sem.at[7], recv_sem[("tz", k % 4)],
+            device_id=dev(x, y, (z + k) % 8, c), device_id_type=MESH).start()
+    for k in (2, 1, 3, 0):
+        landed(got_z.at[pl.ds(0, 2 if k else 1)], ("tz", k))
         first = total[...] if k == 0 else got_z[k]
-        got2[x * 4 + (z + 8 - k) % 4] = first + got_z[k + 4]
-    mine = got2.at[pl.ds(x * 4, 4)]
-    exchange(8, mine, lambda k: mine, [(k, dev((x + k) % 4, y, z, c)) for k in (2, 1, 3)])
+        place = x * 4 + (z + 8 - k) % 4
+        got2[place] = first + got_z[k + 4]
+        mine = got2.at[place]
+        exchange(8, mine, lambda j: mine, [(j, dev((x + j) % 4, y, z, c)) for j in (2, 1, 3)])
     landed(got2.at[pl.ds(0, 12)], ("t", 8))
 
     scores = got2[...]
@@ -422,7 +426,7 @@
         sent(got2.at[pl.ds(0, 4)], 5)
 
 
-N_RECV = 55
+N_RECV = 58
 
 
 def finish(lg, rg, lg_out, rg_out):

time: 50.6 us -> 50.3 us (level)
  no operation moved by 1% of the time
where the time goes in v7:
time: 50.3 us; the launch traced here: 50.1 us
  Pallas kernels  49.5 us (98%)
  between operations  0.64 us (1%)
    pallas_call x1, Pallas kernels, per_device(): pl.pallas_call(kernel, out_shape=(pltpu.VMEM((32, 64), f32), pltpu.VMEM((...  48.8 us

profile of v7, /device:TPU:2, one launch (start us, length us, event | category | flops | bytes accessed | tf_op | source)
XLA Modules:
  0.0 50.1 jit_solution(12147462886438713339)
XLA Ops:
  0.6 48.8 %router_grad.1 = (f32[32,64]{1,0:T(8,128)S(1)}, f32[64,256]{1,0:T(8,128)S(1)}) custom-call(bf16[32,4096]{1,0:T(8,128)(2,1)} %tok.1, bf16[32,4096]{1,0:T(8,128)(2,1)} %cot.1, f32[32,64]{1,0:T(8,128)} %logits.1, s32[8,32]{1,0:T(8,128)} %bitcast.9, bf16[384,4096]{1,0:T(8,128)(2,1)} %bitcast.5, bf16[384,4096]{1,0:T(8,128)(2,1)} %bitcast.6, bf16[384,4096]{1,0:T(8,128)(2,1)} %bitcast.7), custom_call_target="tpu_custom_call" | custom-call | flops 4831838208 | bytes 10485760 | tf_op jit(solution)/shard_map/router_grad/pallas_call | solution.py:441
  49.4 0.6 %finish.1 = (f32[32,64]{1,0:T(8,128)}, f32[64,256]{1,0:T(8,128)}) custom-call(f32[32,64]{1,0:T(8,128)S(1)} %get-tuple-element.6.lg, f32[64,256]{1,0:T(8,128)S(1)} %get-tuple-element.7.rg), custom_call_target="tpu_custom_call" | custom-call | tf_op jit(solution)/shard_map/finish/pallas_call | solution.py:474
